TPU v7x, 32 devices: a whole 2x2x4 slice. The times are simulated.
32 devices in a mesh: seq: 8 (over y, x, core), fsdp: 4 (over z).
Axes of the slice: x: 2, y: 2, z: 4, core: 2. Of those that a mesh axis runs over, the one named last changes fastest.
Arguments:
- tokens: bfloat16 [4, 1024, 768], P('fsdp', 'seq'), may hold values from -6 to 6
- pair_held: int32 [8], replicated, may hold values from 0 to 7, each once
- joint_weight: bfloat16 [768, 2304], P(None, ('seq', 'fsdp')), may hold values from -0.21875 to 0.21875
- joint_bias: bfloat16 [2304], P(('seq', 'fsdp')), may hold values from -3 to 3
- dense_weight: bfloat16 [768, 768], P(('seq', 'fsdp')), may hold values from -3.5 to 3.5
- dense_bias: bfloat16 [768], P(('seq', 'fsdp')), may hold values from -2 to 2
- expand_weight: bfloat16 [768, 3072], P(None, ('seq', 'fsdp')), may hold values from -0.21875 to 0.21875
- expand_bias: bfloat16 [3072], P(('seq', 'fsdp')), may hold values from -3 to 3
- reduce_weight: bfloat16 [3072, 768], P(('seq', 'fsdp')), may hold values from -0.109375 to 0.109375
- reduce_bias: bfloat16 [768], P(('seq', 'fsdp')), may hold values from -2 to 2
- first_gain: bfloat16 [768], P(('seq', 'fsdp')), may hold values from 0.5 to 1.5
- first_shift: bfloat16 [768], P(('seq', 'fsdp')), may hold values from -1 to 1
- second_gain: bfloat16 [768], P(('seq', 'fsdp')), may hold values from 0.5 to 1.5
- second_shift: bfloat16 [768], P(('seq', 'fsdp')), may hold values from -1 to 1
- cotangent: bfloat16 [4, 1024, 768], P('fsdp', 'seq'), may hold values from -6 to 6
Outputs:
- layer_output: bfloat16 [4, 1024, 768], P('fsdp', 'seq')
- input_grad: bfloat16 [4, 1024, 768], P('fsdp', 'seq')
- grad_joint_weight: float32 [768, 2304], P(None, ('seq', 'fsdp'))
- grad_joint_bias: float32 [2304], P(('seq', 'fsdp'))
- grad_dense_weight: float32 [768, 768], P(('seq', 'fsdp'))
- grad_dense_bias: float32 [768], P(('seq', 'fsdp'))
- grad_expand_weight: float32 [768, 3072], P(None, ('seq', 'fsdp'))
- grad_expand_bias: float32 [3072], P(('seq', 'fsdp'))
- grad_reduce_weight: float32 [3072, 768], P(('seq', 'fsdp'))
- grad_reduce_bias: float32 [768], P(('seq', 'fsdp'))
- grad_first_gain: float32 [768], P(('seq', 'fsdp'))
- grad_first_shift: float32 [768], P(('seq', 'fsdp'))
- grad_second_gain: float32 [768], P(('seq', 'fsdp'))
- grad_second_shift: float32 [768], P(('seq', 'fsdp'))
Inputs may be any that keep to these rules, and one draw needn't show every extreme that they name: Index d of seq holds blocks pair_held[d] and 15 - pair_held[d] of every sequence, in that order; every pair is held once.
All inputs are finite; a program needn't handle non-finite values.
Results may differ from a plain program's by a relative error of at most 0.012.
Values may be sent and summed in bfloat16 or wider, within the bound.
A program may use at most 128 MiB of HBM per device.

v0:
```python
import math

import jax
import jax.numpy as jnp
from jax import lax
from jax.sharding import PartitionSpec as P

HD = 64
ROT = 16


norm_eps = 1e-05
masked = -1e30


def layer_norm(values, gain_vec, shift_vec):
    center = values - jnp.mean(values, axis=-1, keepdims=True)
    spread = jnp.mean(center * center, axis=-1, keepdims=True)
    return center * lax.rsqrt(spread + norm_eps) * gain_vec + shift_vec


def row_places(pair_held, offset, count, block_rows):
    pair_count = pair_held.shape[0]
    row_index = offset + jnp.arange(count, dtype=jnp.int32)
    owner_dev = row_index // (2 * block_rows)
    chosen = jnp.sum(
        jnp.where(
            owner_dev[:, None] == jnp.arange(pair_count, dtype=jnp.int32)[None, :],
            pair_held[None, :],
            0,
        ),
        axis=1,
    )
    block_index = jnp.where(row_index // block_rows % 2 == 0, chosen, 2 * pair_count - 1 - chosen)
    return block_index * block_rows + row_index % block_rows


def rotate(values, places):
    half_rot = ROT // 2
    inverse_freq = 1.0 / 10000.0 ** (jnp.arange(0, ROT, 2, dtype=jnp.float32) / ROT)
    angles = places.astype(jnp.float32)[:, None] * inverse_freq[None, :]
    cosine = jnp.cos(angles)[:, None, :]
    sine_term = jnp.sin(angles)[:, None, :]
    lower_half = values[..., :half_rot]
    upper_half = values[..., half_rot:ROT]
    return jnp.concatenate(
        [
            lower_half * cosine - upper_half * sine_term,
            upper_half * cosine + lower_half * sine_term,
            values[..., ROT:],
        ],
        axis=-1,
    )


def rotate_back(grads_in, places):

    def turned(values):
        return rotate(values, places)

    return jax.vjp(turned, grads_in)[1](grads_in)[0]


def gelu_exact(values):
    return jax.nn.gelu(values, approximate=False)


def row_product(left, right):
    return lax.dot_general(
        left, right, (((0,), (0,)), ((), ())), preferred_element_type=jnp.float32
    )


def against(left, right):
    return lax.dot_general(
        left, right, (((1,), (1,)), ((), ())), preferred_element_type=jnp.float32
    )


def body(
    tokens,
    pair_held,
    joint_weight,
    joint_bias,
    dense_weight,
    dense_bias,
    expand_weight,
    expand_bias,
    reduce_weight,
    reduce_bias,
    first_gain,
    first_shift,
    second_gain,
    second_shift,
    cotangent,
):
    weights_all = (
        lax.all_gather(joint_weight, ("seq", "fsdp"), axis=1, tiled=True),
        lax.all_gather(joint_bias, ("seq", "fsdp"), axis=0, tiled=True),
        lax.all_gather(dense_weight, ("seq", "fsdp"), axis=0, tiled=True),
        lax.all_gather(dense_bias, ("seq", "fsdp"), axis=0, tiled=True),
        lax.all_gather(expand_weight, ("seq", "fsdp"), axis=1, tiled=True),
        lax.all_gather(expand_bias, ("seq", "fsdp"), axis=0, tiled=True),
        lax.all_gather(reduce_weight, ("seq", "fsdp"), axis=0, tiled=True),
        lax.all_gather(reduce_bias, ("seq", "fsdp"), axis=0, tiled=True),
        lax.all_gather(first_gain, ("seq", "fsdp"), axis=0, tiled=True),
        lax.all_gather(first_shift, ("seq", "fsdp"), axis=0, tiled=True),
        lax.all_gather(second_gain, ("seq", "fsdp"), axis=0, tiled=True),
        lax.all_gather(second_shift, ("seq", "fsdp"), axis=0, tiled=True),
    )
    seq_count, row_count, features = tokens.shape
    block_rows = row_count // 2
    head_count = features // HD
    score_scale = HD ** (-0.5)
    my_places = row_places(pair_held, lax.axis_index("seq") * row_count, row_count, block_rows)
    inputs_flat = tokens.astype(jnp.float32).reshape(seq_count * row_count, features)
    normed_first = layer_norm(
        inputs_flat, weights_all[8].astype(jnp.float32), weights_all[9].astype(jnp.float32)
    ).astype(jnp.bfloat16)
    projected = jnp.dot(
        normed_first, weights_all[0], preferred_element_type=jnp.float32
    ) + weights_all[1].astype(jnp.float32)
    projected = projected.reshape(seq_count, row_count, head_count, 3, HD)
    queries = rotate(projected[:, :, :, 0], my_places).astype(jnp.bfloat16)
    keys_local = (
        rotate(projected[:, :, :, 1], my_places)
        .astype(jnp.bfloat16)
        .reshape(seq_count, row_count, features)
    )
    values_local = (
        projected[:, :, :, 2].astype(jnp.bfloat16).reshape(seq_count, row_count, features)
    )
    start_state = (
        jnp.full((seq_count, head_count, row_count), masked, jnp.float32),
        jnp.zeros((seq_count, head_count, row_count), jnp.float32),
        jnp.zeros((seq_count, head_count, row_count, HD), jnp.float32),
    )
    key_piece = lax.all_gather(keys_local, "seq", axis=1, tiled=True)
    value_piece = lax.all_gather(values_local, "seq", axis=1, tiled=True)
    piece_rows = key_piece.shape[1]
    fold_key_span = math.gcd(piece_rows, 512)

    def key_step(state_now, step_index):
        old_peak, running_sum, accumulated = state_now
        offset = step_index * fold_key_span
        key_block = lax.dynamic_slice_in_dim(key_piece, offset, fold_key_span, 1).reshape(
            seq_count, fold_key_span, head_count, HD
        )
        value_block = lax.dynamic_slice_in_dim(value_piece, offset, fold_key_span, 1).reshape(
            seq_count, fold_key_span, head_count, HD
        )
        allowed = (
            my_places[:, None] >= row_places(pair_held, offset, fold_key_span, block_rows)[None, :]
        )
        scores = (
            jnp.einsum("sqhd,skhd->shqk", queries, key_block, preferred_element_type=jnp.float32)
            * score_scale
        )
        scores = jnp.where(allowed, scores, masked)
        new_peak = jnp.maximum(old_peak, jnp.max(scores, axis=-1))
        weight = jnp.where(allowed, jnp.exp(scores - new_peak[..., None]), 0.0)
        shrink = jnp.exp(old_peak - new_peak)
        running_sum = running_sum * shrink + jnp.sum(weight, axis=-1)
        accumulated = accumulated * shrink[..., None] + jnp.einsum(
            "shqk,skhd->shqd",
            weight.astype(jnp.bfloat16),
            value_block,
            preferred_element_type=jnp.float32,
        )
        return ((new_peak, running_sum, accumulated), None)

    state_out, unused = lax.scan(
        key_step, start_state, jnp.arange(piece_rows // fold_key_span, dtype=jnp.int32)
    )
    final_peak, final_sum, accumulated = state_out
    log_total = final_peak + jnp.log(final_sum)
    context_heads = jnp.moveaxis(accumulated / final_sum[..., None], 1, 2)
    context_low = context_heads.reshape(seq_count * row_count, features).astype(jnp.bfloat16)
    branch_attn = jnp.dot(
        context_low, weights_all[2], preferred_element_type=jnp.float32
    ) + weights_all[3].astype(jnp.float32)
    normed_second = layer_norm(
        inputs_flat, weights_all[10].astype(jnp.float32), weights_all[11].astype(jnp.float32)
    ).astype(jnp.bfloat16)
    hidden = jnp.dot(
        normed_second, weights_all[4], preferred_element_type=jnp.float32
    ) + weights_all[5].astype(jnp.float32)
    active, gelu_pull = jax.vjp(gelu_exact, hidden)
    active_low = active.astype(jnp.bfloat16)
    branch_mlp = jnp.dot(
        active_low, weights_all[6], preferred_element_type=jnp.float32
    ) + weights_all[7].astype(jnp.float32)
    layer_output = (
        (inputs_flat + branch_attn + branch_mlp)
        .astype(jnp.bfloat16)
        .reshape(seq_count, row_count, features)
    )
    back_weights = (
        lax.all_gather(joint_weight, ("seq", "fsdp"), axis=1, tiled=True),
        lax.all_gather(joint_bias, ("seq", "fsdp"), axis=0, tiled=True),
        lax.all_gather(dense_weight, ("seq", "fsdp"), axis=0, tiled=True),
        lax.all_gather(dense_bias, ("seq", "fsdp"), axis=0, tiled=True),
        lax.all_gather(expand_weight, ("seq", "fsdp"), axis=1, tiled=True),
        lax.all_gather(expand_bias, ("seq", "fsdp"), axis=0, tiled=True),
        lax.all_gather(reduce_weight, ("seq", "fsdp"), axis=0, tiled=True),
        lax.all_gather(reduce_bias, ("seq", "fsdp"), axis=0, tiled=True),
        lax.all_gather(first_gain, ("seq", "fsdp"), axis=0, tiled=True),
        lax.all_gather(first_shift, ("seq", "fsdp"), axis=0, tiled=True),
        lax.all_gather(second_gain, ("seq", "fsdp"), axis=0, tiled=True),
        lax.all_gather(second_shift, ("seq", "fsdp"), axis=0, tiled=True),
    )
    upstream = cotangent.reshape(seq_count * row_count, features)
    upstream_f = upstream.astype(jnp.float32)
    grad_out_bias = jnp.sum(upstream_f, axis=0)
    g_hidden = gelu_pull(against(upstream, back_weights[6]))[0].astype(jnp.bfloat16)
    g_second = against(g_hidden, back_weights[4])
    g_context = (
        against(upstream, back_weights[2])
        .astype(jnp.bfloat16)
        .reshape(seq_count, row_count, head_count, HD)
    )
    row_delta = jnp.moveaxis(jnp.sum(g_context.astype(jnp.float32) * context_heads, axis=-1), 1, 2)
    keys_all, values_all = (
        lax.all_gather(keys_local, "seq", axis=1, tiled=True),
        lax.all_gather(values_local, "seq", axis=1, tiled=True),
    )
    length = keys_all.shape[1]
    key_span = math.gcd(length, 512)

    def query_step(step_index, g_queries):
        offset = step_index * key_span
        key_block = lax.dynamic_slice_in_dim(keys_all, offset, key_span, 1).reshape(
            seq_count, key_span, head_count, HD
        )
        value_block = lax.dynamic_slice_in_dim(values_all, offset, key_span, 1).reshape(
            seq_count, key_span, head_count, HD
        )
        allowed = my_places[:, None] >= row_places(pair_held, offset, key_span, block_rows)[None, :]
        scores = (
            jnp.einsum("sqhd,skhd->shqk", queries, key_block, preferred_element_type=jnp.float32)
            * score_scale
        )
        probs_full = jnp.where(allowed, jnp.exp(scores - log_total[..., None]), 0.0)
        g_probs = jnp.einsum(
            "sqhd,skhd->shqk", g_context, value_block, preferred_element_type=jnp.float32
        )
        g_scores = (probs_full * (g_probs - row_delta[..., None])).astype(jnp.bfloat16)
        return (
            g_queries
            + jnp.einsum("shqk,skhd->sqhd", g_scores, key_block, preferred_element_type=jnp.float32)
            * score_scale
        )

    g_queries = lax.fori_loop(
        0,
        length // key_span,
        query_step,
        jnp.zeros((seq_count, row_count, head_count, HD), jnp.float32),
    )
    queries_all, g_context_all = (
        lax.all_gather(queries, "seq", axis=1, tiled=True),
        lax.all_gather(g_context, "seq", axis=1, tiled=True),
    )
    log_all, delta_all = (
        lax.all_gather(log_total, "seq", axis=2, tiled=True),
        lax.all_gather(row_delta, "seq", axis=2, tiled=True),
    )
    own_keys = keys_local.reshape(seq_count, row_count, head_count, HD)
    own_values = values_local.reshape(seq_count, row_count, head_count, HD)

    def owner_step(step_index, state_now):
        g_keys, g_values = state_now
        offset = step_index * key_span
        query_block = lax.dynamic_slice_in_dim(queries_all, offset, key_span, 1)
        context_block = lax.dynamic_slice_in_dim(g_context_all, offset, key_span, 1)
        log_block = lax.dynamic_slice_in_dim(log_all, offset, key_span, 2)
        delta_block = lax.dynamic_slice_in_dim(delta_all, offset, key_span, 2)
        allowed = row_places(pair_held, offset, key_span, block_rows)[:, None] >= my_places[None, :]
        scores = (
            jnp.einsum("sqhd,skhd->shqk", query_block, own_keys, preferred_element_type=jnp.float32)
            * score_scale
        )
        probs_full = jnp.where(allowed, jnp.exp(scores - log_block[..., None]), 0.0)
        g_probs = jnp.einsum(
            "sqhd,skhd->shqk", context_block, own_values, preferred_element_type=jnp.float32
        )
        g_scores = (probs_full * (g_probs - delta_block[..., None])).astype(jnp.bfloat16)
        g_keys = (
            g_keys
            + jnp.einsum(
                "shqk,sqhd->skhd", g_scores, query_block, preferred_element_type=jnp.float32
            )
            * score_scale
        )
        g_values = g_values + jnp.einsum(
            "shqk,sqhd->skhd",
            probs_full.astype(jnp.bfloat16),
            context_block,
            preferred_element_type=jnp.float32,
        )
        return (g_keys, g_values)

    owner_start = (
        jnp.zeros((seq_count, row_count, head_count, HD), jnp.float32),
        jnp.zeros((seq_count, row_count, head_count, HD), jnp.float32),
    )
    own_gk, own_gv = lax.fori_loop(0, length // key_span, owner_step, owner_start)
    g_query_raw = rotate_back(g_queries, my_places)
    g_key_raw = rotate_back(own_gk, my_places)
    g_projected = (
        jnp.stack([g_query_raw, g_key_raw, own_gv], axis=3)
        .reshape(seq_count * row_count, 3 * features)
        .astype(jnp.bfloat16)
    )
    g_first = against(g_projected, back_weights[0])
    unused_first, norm_pull_first = jax.vjp(
        layer_norm,
        inputs_flat,
        back_weights[8].astype(jnp.float32),
        back_weights[9].astype(jnp.float32),
    )
    g_input_first, grad_first_gain, grad_first_shift = norm_pull_first(g_first)
    unused_second, norm_pull_second = jax.vjp(
        layer_norm,
        inputs_flat,
        back_weights[10].astype(jnp.float32),
        back_weights[11].astype(jnp.float32),
    )
    g_input_second, grad_second_gain, grad_second_shift = norm_pull_second(g_second)
    input_grad = (
        (upstream_f + g_input_first + g_input_second)
        .astype(jnp.bfloat16)
        .reshape(seq_count, row_count, features)
    )
    rows_all = (
        lax.all_gather(normed_first, "seq", axis=0, tiled=True),
        lax.all_gather(normed_second, "seq", axis=0, tiled=True),
        lax.all_gather(upstream, "seq", axis=0, tiled=True),
    )
    columns = (
        lax.all_to_all(g_projected, "seq", split_axis=1, concat_axis=0, tiled=True),
        lax.all_to_all(g_hidden, "seq", split_axis=1, concat_axis=0, tiled=True),
        lax.all_to_all(context_low, "seq", split_axis=1, concat_axis=0, tiled=True),
        lax.all_to_all(active_low, "seq", split_axis=1, concat_axis=0, tiled=True),
    )
    joint_term = row_product(rows_all[0], columns[0])
    joint_bias_term = jnp.sum(columns[0].astype(jnp.float32), axis=0)
    expand_term = row_product(rows_all[1], columns[1])
    expand_bias_term = jnp.sum(columns[1].astype(jnp.float32), axis=0)
    dense_term = row_product(columns[2], rows_all[2])
    reduce_term = row_product(columns[3], rows_all[2])
    vectors = (
        lax.psum_scatter(grad_out_bias, "seq", scatter_dimension=0, tiled=True),
        lax.psum_scatter(grad_first_gain, "seq", scatter_dimension=0, tiled=True),
        lax.psum_scatter(grad_first_shift, "seq", scatter_dimension=0, tiled=True),
        lax.psum_scatter(grad_second_gain, "seq", scatter_dimension=0, tiled=True),
        lax.psum_scatter(grad_second_shift, "seq", scatter_dimension=0, tiled=True),
    )
    owned_grads = (
        lax.psum_scatter(
            joint_term.astype(jnp.bfloat16), "fsdp", scatter_dimension=1, tiled=True
        ).astype(jnp.float32),
        lax.psum_scatter(
            joint_bias_term.astype(jnp.bfloat16), "fsdp", scatter_dimension=0, tiled=True
        ).astype(jnp.float32),
        lax.psum_scatter(
            dense_term.astype(jnp.bfloat16), "fsdp", scatter_dimension=0, tiled=True
        ).astype(jnp.float32),
        lax.psum_scatter(
            vectors[0].astype(jnp.bfloat16), "fsdp", scatter_dimension=0, tiled=True
        ).astype(jnp.float32),
        lax.psum_scatter(
            expand_term.astype(jnp.bfloat16), "fsdp", scatter_dimension=1, tiled=True
        ).astype(jnp.float32),
        lax.psum_scatter(
            expand_bias_term.astype(jnp.bfloat16), "fsdp", scatter_dimension=0, tiled=True
        ).astype(jnp.float32),
        lax.psum_scatter(
            reduce_term.astype(jnp.bfloat16), "fsdp", scatter_dimension=0, tiled=True
        ).astype(jnp.float32),
        lax.psum_scatter(
            vectors[0].astype(jnp.bfloat16), "fsdp", scatter_dimension=0, tiled=True
        ).astype(jnp.float32),
        lax.psum_scatter(
            vectors[1].astype(jnp.bfloat16), "fsdp", scatter_dimension=0, tiled=True
        ).astype(jnp.float32),
        lax.psum_scatter(
            vectors[2].astype(jnp.bfloat16), "fsdp", scatter_dimension=0, tiled=True
        ).astype(jnp.float32),
        lax.psum_scatter(
            vectors[3].astype(jnp.bfloat16), "fsdp", scatter_dimension=0, tiled=True
        ).astype(jnp.float32),
        lax.psum_scatter(
            vectors[4].astype(jnp.bfloat16), "fsdp", scatter_dimension=0, tiled=True
        ).astype(jnp.float32),
    )
    return (
        layer_output,
        input_grad,
        owned_grads[0],
        owned_grads[1],
        owned_grads[2],
        owned_grads[3],
        owned_grads[4],
        owned_grads[5],
        owned_grads[6],
        owned_grads[7],
        owned_grads[8],
        owned_grads[9],
        owned_grads[10],
        owned_grads[11],
    )


def solution(mesh):
    placed = (
        P("fsdp", "seq", None),
        P(),
        P(None, ("seq", "fsdp")),
        P(("seq", "fsdp")),
        P(("seq", "fsdp"), None),
        P(("seq", "fsdp")),
        P(None, ("seq", "fsdp")),
        P(("seq", "fsdp")),
        P(("seq", "fsdp"), None),
        P(("seq", "fsdp")),
        P(("seq", "fsdp")),
        P(("seq", "fsdp")),
        P(("seq", "fsdp")),
        P(("seq", "fsdp")),
        P("fsdp", "seq", None),
    )
    return jax.shard_map(
        body,
        mesh=mesh,
        in_specs=placed,
        out_specs=(
            P("fsdp", "seq", None),
            P("fsdp", "seq", None),
            P(None, ("seq", "fsdp")),
            P(("seq", "fsdp")),
            P(("seq", "fsdp"), None),
            P(("seq", "fsdp")),
            P(None, ("seq", "fsdp")),
            P(("seq", "fsdp")),
            P(("seq", "fsdp"), None),
            P(("seq", "fsdp")),
            P(("seq", "fsdp")),
            P(("seq", "fsdp")),
            P(("seq", "fsdp")),
            P(("seq", "fsdp")),
        ),
        check_vma=False,
    )
```

profile of v0, /device:TPU:0, one launch (start us, length us, event | category | flops | bytes accessed | tf_op | source)
XLA Modules:
  0.0 553.6 jit_solution(6225122801599621082)
XLA Ops:
  16.8 42.7 %all-reduce.27 = (bf16[768]{0:T(1024)(128)(2,1)S(1)}, bf16[768]{0:T(1024)(128)(2,1)S(1)}, bf16[3072]{0:T(1024)(128)(2,1)S(1)}, bf16[768]{0:T(1024)(128)(2,1)S(1)...) all-reduce(bf16[768]{0:T(1024)(128)(2,1)S(1)} %dynamic-update-slice, ...), channel_id=1, replica_groups=mesh['seq'=8,'fsdp'=4] {'seq','fsdp'}, use_global_device_ids=true, to_apply=%add.11 | all-reduce | flops 9984 | bytes 39936
  61.3 1.1 fusion.128
  63.2 1.8 fusion.123
  65.0 8.8 %all-gather.13.cloned.1.call-done = bf16[768,2304]{0,1:T(8,128)(2,1)} async-done(((bf16[768,72]{0,1:T(8,128)(2,1)}), bf16[768,2304]{0,1:T(8,128)(2,1)}) %all-gather.13.cloned.1.call-update) | async-done | bytes 3538960 | tf_op jit(solution)/shard_map/all_gather | solution.py:98
  73.8 3.3 convolution_add_fusion
  79.2 50.3 %all-gather.19.cloned.1.call-done = bf16[768,768]{1,0:T(8,128)(2,1)} async-done(((bf16[24,768]{1,0:T(8,128)(2,1)}), bf16[768,768]{1,0:T(8,128)(2,1)}) %all-gather.19.cloned.1.call-update) | async-done | bytes 1179664 | tf_op jit(solution)/shard_map/all_gather | solution.py:100
  129.5 1.8 convolution_convert_fusion.2
  140.2 54.6 %all-gather.21.cloned.1.call-done = bf16[768,3072]{0,1:T(8,128)(2,1)} async-done(((bf16[768,96]{0,1:T(8,128)(2,1)}), bf16[768,3072]{0,1:T(8,128)(2,1)}) %all-gather.21.cloned.1.call-update) | async-done | bytes 4718608 | tf_op jit(solution)/shard_map/all_gather | solution.py:102
  194.8 7.9 %multiply_convert_fusion.1 = (bf16[128,3072]{1,0:T(8,128)(2,1)S(1)}, f32[128,3072]{1,0:T(8,128)S(1)}, f32[128,3072]{1,0:T(8,128)}) fusion(f32[3072]{0:T(1024)S(1)} %convert_element_type.274, bf16[128,768]{1,0:T(8,128)(2,1)S(1)} %copy-done.18, bf16[768,3072]{0,1:T(8,128)(2,1)} %all-gather.21.cloned.1.call-done), kind=kOutput, calls=%fused_computation.151 | convolution fusion | flops 629932032 | bytes 8859648 | tf_op jit(solution)/shard_map/dot_general | solution.py:185
  202.8 57.1 %all-gather.23.cloned.1.call-done = bf16[3072,768]{1,0:T(8,128)(2,1)} async-done(((bf16[96,768]{1,0:T(8,128)(2,1)}), bf16[3072,768]{1,0:T(8,128)(2,1)}) %all-gather.23.cloned.1.call-update) | async-done | bytes 4718608 | tf_op jit(solution)/shard_map/all_gather | solution.py:104
  259.9 4.8 add_convert_fusion
  264.6 1.1 copy.91
  266.8 1.6 fusion.154
  269.4 1.6 convolution_add_fusion.3
  270.9 16.0 %all-gather.15.cloned.1.call-done = bf16[1,1024,768]{1,2,0:T(8,128)(2,1)} async-done(((bf16[1,128,768]{1,2,0:T(8,128)(2,1)}), bf16[1,1024,768]{1,2,0:T(8,128)(2,1)}) %all-gather.15.cloned.1.call-update) | async-done | bytes 1572880 | tf_op jit(solution)/shard_map/all_gather | solution.py:138
  286.9 28.2 %all-gather.17.cloned.1.call-done = bf16[1,1024,768]{1,2,0:T(8,128)(2,1)} async-done(((bf16[1,128,768]{1,2,0:T(8,128)(2,1)}), bf16[1,1024,768]{1,2,0:T(8,128)(2,1)}) %all-gather.17.cloned.1.call-update) | async-done | bytes 1572880 | tf_op jit(solution)/shard_map/all_gather | solution.py:139
  315.1 18.2 %while.54 = (s32[]{:T(128)}, f32[1,12,128]{2,1,0:T(8,128)S(1)}, f32[1,12,128]{2,1,0:T(8,128)S(1)}, f32[1,12,128,64]{2,3,1,0:T(8,128)}, s32[128]{0:T(128)}, /*ind...) while((s32[]{:T(128)}, f32[1,12,128]{2,1,0:T(8,128)S(1)}, ...), condition=%wide.region_7.8_spmd.clone, body=%wide.region_3.7_spmd.clone.sunk | while | flops 211958272 | bytes 15512311 | solution.py:172
  316.4 2.4 constant_dynamic-slice_fusion.6
  320.5 2.9 fusion.214
  325.4 2.4 constant_dynamic-slice_fusion.6
  329.5 3.0 fusion.214
  333.3 1.2 fusion.133
  334.5 1.8 bitcast_convert_fusion
  336.3 10.1 %all_gather.88 = f32[1,12,1024]{2,1,0:T(8,128)} all-gather(f32[1,12,128]{2,1,0:T(8,128)S(1)} %bitcast.365), channel_id=1, replica_groups=mesh['seq'=8,'fsdp'=4] {'seq'}, dimensions={2}, use_global_device_ids=true | all-gather | bytes 55296 | tf_op jit(solution)/shard_map/all_gather | solution.py:266
  346.4 9.1 %all_gather.86 = f32[1,12,1024]{2,1,0:T(8,128)} all-gather(f32[1,12,128]{2,1,0:T(8,128)S(1)} %log_add_fusion), channel_id=1, replica_groups=mesh['seq'=8,'fsdp'=4] {'seq'}, dimensions={2}, use_global_device_ids=true | all-gather | bytes 55296 | tf_op jit(solution)/shard_map/all_gather | solution.py:265
  355.5 4.3 all-to-all-start.1
  359.8 12.2 %all-gather.25.cloned.1.call-done = bf16[1,1024,12,64]{1,3,2,0:T(8,128)(2,1)} async-done(((bf16[1,128,12,64]{1,3,2,0:T(8,128)(2,1)}), bf16[1,1024,12,64]{1,3,2,0:T(8,128)(2,1)}) %all-gather.25.cloned.1.call-update) | async-done | bytes 1572880 | tf_op jit(solution)/shard_map/all_gather | solution.py:261
  372.0 23.7 %while.56 = (s32[]{:T(128)}, f32[1,128,12,64]{1,3,2,0:T(8,128)}, f32[1,128,12,64]{1,3,2,0:T(8,128)}, bf16[1,1024,12,64]{1,3,2,0:T(8,128)(2,1)}, s32[8]{0:T(128)}...) while((s32[]{:T(128)}, f32[1,128,12,64]{1,3,2,0:T(8,128)}, ...), condition=%wide.region_14.15_spmd.clone, body=%wide.region_12.14_spmd.clone.sunk | while | flops 411112960 | bytes 15350221 | solution.py:307
  372.1 1.8 fusion.230
  374.7 1.4 broadcast_compare_fusion.8
  376.1 3.0 fusion.233
  379.1 4.6 fusion.232
  383.7 1.8 fusion.230
  386.3 1.4 broadcast_compare_fusion.8
  387.7 3.1 fusion.233
  390.8 5.0 fusion.232
  395.8 4.4 all-to-all-start.2
  400.2 17.0 %while.55 = (s32[]{:T(128)}, f32[1,128,12,64]{1,3,2,0:T(8,128)}, bf16[1,1024,768]{1,2,0:T(8,128)(2,1)}, s32[128]{0:T(128)}, s32[8]{0:T(128)S(1)}, /*index=5*/bf1...) while((s32[]{:T(128)}, f32[1,128,12,64]{1,3,2,0:T(8,128)}, ...), condition=%wide.region_11.12_spmd.clone, body=%wide.region_9.11_spmd.clone.sunk | while | flops 307107328 | bytes 16278277 | solution.py:254
  400.2 2.4 constant_dynamic-slice_fusion.7
  403.6 1.4 broadcast_compare_fusion.7
  405.0 3.6 fusion.222
  408.6 2.4 constant_dynamic-slice_fusion.7
  412.1 1.4 broadcast_compare_fusion.7
  413.5 3.8 fusion.222
  417.2 2.6 fusion.105
  419.8 4.1 all-to-all-start.3
  424.0 3.8 all-gather.31.cloned.1.call-done
  427.8 3.4 convolution_convert_fusion
  433.7 2.7 fusion.150
  436.5 4.2 all-to-all-start
  440.8 2.9 fusion.99
  443.8 2.2 fusion.108
  446.4 10.2 %all-gather.29.cloned.1.call-done = bf16[1024,768]{1,0:T(8,128)(2,1)} async-done(((bf16[128,768]{1,0:T(8,128)(2,1)}), bf16[1024,768]{1,0:T(8,128)(2,1)}) %all-gather.29.cloned.1.call-update) | async-done | bytes 1572880 | tf_op jit(solution)/shard_map/all_gather | solution.py:336
  456.7 3.0 convolution_convert_fusion.1
  460.7 22.7 %all-reduce.26 = (bf16[768]{0:T(1024)(128)(2,1)S(1)}, bf16[768]{0:T(1024)(128)(2,1)S(1)}, bf16[768]{0:T(1024)(128)(2,1)S(1)}, bf16[768]{0:T(1024)(128)(2,1)S(1)}, bf16[768]{0:T(1024)(128)(2,1)S(1)}) all-reduce(f32[768]{0:T(1024)S(1)} %get-tuple-element.1053, ...), channel_id=6, replica_groups=mesh['seq'=8,'fsdp'=4] {'seq'}, use_global_device_ids=true, to_apply=%region_24.25.clone | all-reduce | flops 3840 | bytes 23040
  483.8 1.3 reduce_sum.268
  485.2 1.4 convert_element_type.292
  486.6 1.2 reduce_sum.266
  487.8 12.1 %all-reduce.28 = (bf16[288]{0:T(512)(128)(2,1)S(1)}, bf16[96]{0:T(256)(128)(2,1)S(1)}, bf16[384]{0:T(512)(128)(2,1)S(1)}, bf16[96]{0:T(256)(128)(2,1)S(1)}, bf16...) all-reduce(bf16[288]{0:T(512)(128)(2,1)S(1)} %reduce_sum.266, ...), channel_id=4, replica_groups=mesh['seq'=8,'fsdp'=4] {'fsdp'}, use_global_device_ids=true, to_apply=%region_21.22.clone | all-reduce | flops 1152 | bytes 4608
  503.5 1.6 convert_element_type.296
  505.1 18.1 %reduce-scatter.11.cloned.1.call-done = bf16[96,768]{1,0:T(8,128)(2,1)} async-done(((bf16[384,768]{1,0:T(8,128)(2,1)}), bf16[96,768]{1,0:T(8,128)(2,1)}) %reduce-scatter.11.cloned.1.call-update) | async-done | bytes 147472 | tf_op jit(solution)/shard_map/reduce_scatter | solution.py:378
  523.2 1.6 convert_element_type.299
  524.9 20.1 %reduce-scatter.5.cloned.1.call-done = bf16[768,72]{0,1:T(8,128)(2,1)} async-done(((bf16[768,288]{0,1:T(8,128)(2,1)}), bf16[768,72]{0,1:T(8,128)(2,1)}) %reduce-scatter.5.cloned.1.call-update) | async-done | bytes 110608 | tf_op jit(solution)/shard_map/reduce_scatter | solution.py:360
  545.0 1.6 convert_element_type.288
  (258 shorter events, 40.7 us)
Async XLA Ops:
  7.2 66.6 %all-gather.13.cloned.1.call-start = ((), (), s32[]{:S(2)}) async-start(), calls=%async_computation.8 | async-start | bytes 3649536 | tf_op jit(solution)/shard_map/all_gather | solution.py:98
  7.9 121.6 %all-gather.19.cloned.1.call-start = ((), (), s32[]{:S(2)}) async-start(), calls=%async_computation.11 | async-start | bytes 1216512 | tf_op jit(solution)/shard_map/all_gather | solution.py:100
  8.7 186.1 %all-gather.21.cloned.1.call-start = ((), (), s32[]{:S(2)}) async-start(), calls=%async_computation.12 | async-start | bytes 4866048 | tf_op jit(solution)/shard_map/all_gather | solution.py:102
  9.4 250.5 %all-gather.23.cloned.1.call-start = ((), (), s32[]{:S(2)}) async-start(), calls=%async_computation.13 | async-start | bytes 4866048 | tf_op jit(solution)/shard_map/all_gather | solution.py:104
  10.0 276.9 %all-gather.15.cloned.1.call-start = ((), (), s32[]{:S(2)}) async-start(), calls=%async_computation.9 | async-start | bytes 1769472 | tf_op jit(solution)/shard_map/all_gather | solution.py:138
  59.4 14.3 %copy-start.25 = (f32[768]{0:T(1024)}, f32[768]{0:T(1024)S(1)}, u32[]{:S(2)}) copy-start(f32[768]{0:T(1024)S(1)} %convert_element_type.259) | copy-start | bytes 9220
  59.4 14.3 %copy-start.27 = (f32[768]{0:T(1024)}, f32[768]{0:T(1024)S(1)}, u32[]{:S(2)}) copy-start(f32[768]{0:T(1024)S(1)} %convert_element_type.271) | copy-start | bytes 9220
  61.3 12.4 %copy-start.37 = (f32[128]{0:T(128)}, f32[128]{0:T(128)S(1)}, u32[]{:S(2)}) copy-start(f32[128]{0:T(128)S(1)} %broadcast_multiply_fusion) | copy-start | bytes 1540
  62.5 14.6 %copy-start.41 = (f32[128]{0:T(128)}, f32[128]{0:T(128)S(1)}, u32[]{:S(2)}) copy-start(f32[128]{0:T(128)S(1)} %fusion.128) | copy-start | bytes 1540
  62.5 14.6 %copy-start.39 = (f32[128]{0:T(128)}, f32[128]{0:T(128)S(1)}, u32[]{:S(2)}) copy-start(f32[128]{0:T(128)S(1)} %fusion.146) | copy-start | bytes 1540
  63.1 69.1 %copy-start.29 = (f32[128,8]{0,1:T(8,128)}, f32[128,8]{0,1:T(8,128)S(1)}, u32[]{:S(2)}) copy-start(f32[128,8]{0,1:T(8,128)S(1)} %get-tuple-element.1057) | copy-start | bytes 12292
  63.1 69.1 %copy-start.31 = (f32[128,8]{0,1:T(8,128)}, f32[128,8]{0,1:T(8,128)S(1)}, u32[]{:S(2)}) copy-start(f32[128,8]{0,1:T(8,128)S(1)} %get-tuple-element.1058) | copy-start | bytes 12292
  65.0 12.1 %copy-start.11 = (bf16[128,768]{1,0:T(8,128)(2,1)}, bf16[128,768]{1,0:T(8,128)(2,1)S(1)}, u32[]{:S(2)}) copy-start(bf16[128,768]{1,0:T(8,128)(2,1)S(1)} %get-tuple-element.1049) | copy-start | bytes 589828
  77.5 52.0 %copy-start.12 = (bf16[1,128,768]{2,1,0:T(8,128)(2,1)S(1)}, bf16[1,128,768]{2,1,0:T(8,128)(2,1)}, u32[]{:S(2)}) copy-start(bf16[1,128,768]{2,1,0:T(8,128)(2,1)} %param.35) | copy-start | bytes 589828
  78.3 236.8 %all-gather.17.cloned.1.call-start = ((), (), s32[]{:S(2)}) async-start(), calls=%async_computation.10 | async-start | bytes 1769472 | tf_op jit(solution)/shard_map/all_gather | solution.py:139
  79.1 56.0 %copy-start.44 = (u32[32]{0:T(128)S(1)}, u32[32]{0:T(128)}, u32[]{:S(2)}) copy-start(u32[32]{0:T(128)} %constant.734) | copy-start | bytes 388
  79.1 56.6 %copy-start.43 = (u32[32]{0:T(128)S(1)}, u32[32]{0:T(128)}, u32[]{:S(2)}) copy-start(u32[32]{0:T(128)} %constant.730) | copy-start | bytes 388
  79.1 280.7 %all-gather.27.cloned.1.call-start = ((), (), s32[]{:S(2)}) async-start(), calls=%async_computation.15 | async-start | bytes 1769472 | tf_op jit(solution)/shard_map/all_gather | solution.py:262
  131.3 63.5 %copy-start.18 = (bf16[128,768]{1,0:T(8,128)(2,1)S(1)}, bf16[128,768]{1,0:T(8,128)(2,1)}, u32[]{:S(2)}) copy-start(bf16[128,768]{1,0:T(8,128)(2,1)} %get-tuple-element.1050) | copy-start | bytes 589828
  132.1 239.9 %all-gather.25.cloned.1.call-start = ((), (), s32[]{:S(2)}) async-start(), calls=%async_computation.14 | async-start | bytes 1769472 | tf_op jit(solution)/shard_map/all_gather | solution.py:261
  133.0 284.2 %all-gather.33.cloned.1.call-start = ((), (), s32[]{:S(2)}) async-start(), calls=%async_computation.22 | async-start | bytes 1769472 | tf_op jit(solution)/shard_map/all_gather | solution.py:338
  133.7 294.0 %all-gather.31.cloned.1.call-start = ((), (), s32[]{:S(2)}) async-start(), calls=%async_computation.19 | async-start | bytes 1769472 | tf_op jit(solution)/shard_map/all_gather | solution.py:337
  134.3 322.3 %all-gather.29.cloned.1.call-start = ((), (), s32[]{:S(2)}) async-start(), calls=%async_computation.16 | async-start | bytes 1769472 | tf_op jit(solution)/shard_map/all_gather | solution.py:336
  140.2 119.6 %copy-start.13 = (bf16[1,128,768]{2,1,0:T(8,128)(2,1)S(1)}, bf16[1,128,768]{2,1,0:T(8,128)(2,1)}, u32[]{:S(2)}) copy-start(bf16[1,128,768]{2,1,0:T(8,128)(2,1)} %param.35) | copy-start | bytes 589828
  259.9 6.9 %slice-start = ((s8[4718592]{0:T(1024)(128)(4,1)}), s8[4194304]{0:T(1024)(128)(4,1)S(1)}, s32[]{:S(2)}) async-start(s8[4718592]{0:T(1024)(128)(4,1)} %bitcast.350), calls=%async_computation.23 | async-start | bytes 8388608
  259.9 6.9 %slice-start.1 = ((s8[4718592]{0:T(1024)(128)(4,1)}), s8[524288]{0:T(1024)(128)(4,1)S(1)}, s32[]{:S(2)}) async-start(s8[4718592]{0:T(1024)(128)(4,1)} %bitcast.350), calls=%async_computation.24 | async-start | bytes 1048576
  266.8 2.6 copy-start.7
  269.4 45.8 %copy-start.1 = (bf16[1,128,12,64]{1,3,2,0:T(8,128)(2,1)S(1)}, bf16[1,128,12,64]{1,3,2,0:T(8,128)(2,1)}, u32[]{:S(2)}) copy-start(bf16[1,128,12,64]{1,3,2,0:T(8,128)(2,1)} %pad_maximum_fusion) | copy-start | bytes 589828
  269.4 45.8 %copy-start.22 = (s32[8]{0:T(128)S(1)}, s32[8]{0:T(128)}, u32[]{:S(2)}) copy-start(s32[8]{0:T(128)} %param.22) | copy-start | bytes 100
  333.3 38.7 %copy-start.3 = (bf16[1,128,12,64]{1,3,2,0:T(8,128)(2,1)S(1)}, bf16[1,128,12,64]{1,3,2,0:T(8,128)(2,1)}, u32[]{:S(2)}) copy-start(bf16[1,128,12,64]{1,3,2,0:T(8,128)(2,1)} %maximum_convert_fusion.1) | copy-start | bytes 589828
  334.5 37.5 %copy-start.33 = (f32[128,12]{0,1:T(8,128)}, f32[128,12]{0,1:T(8,128)S(1)}, u32[]{:S(2)}) copy-start(f32[128,12]{0,1:T(8,128)S(1)} %fusion.133) | copy-start | bytes 18436
  336.3 35.7 %copy-start.35 = (f32[1,12,128]{2,1,0:T(8,128)}, f32[1,12,128]{2,1,0:T(8,128)S(1)}, u32[]{:S(2)}) copy-start(f32[1,12,128]{2,1,0:T(8,128)S(1)} %log_add_fusion) | copy-start | bytes 18436
  355.5 40.2 %all-to-all-start.1 = ((bf16[128,8,96]{0,2,1:T(8,128)(2,1)}), bf16[128,8,96]{0,2,1:T(8,128)(2,1)}, u32[]{:S(2)}, u32[]{:S(2)}) async-start(bf16[128,8,96]{0,2,1:T(8,128)(2,1)} %bitcast.23), calls=%async_computation.2 | async-start | bytes 393216 | tf_op jit(solution)/shard_map/all_to_all | solution.py:343
  372.0 1.9 copy-start.17
  372.0 2.5 copy-start.23
  383.6 2.5 copy-start.23
  395.7 4.4 copy-start.15
  395.7 4.4 copy-start.24
  395.7 4.4 copy-start.34
  395.8 24.1 %all-to-all-start.2 = ((bf16[128,8,384]{2,0,1:T(8,128)(2,1)}), bf16[128,8,384]{2,0,1:T(8,128)(2,1)}, u32[]{:S(2)}, u32[]{:S(2)}) async-start(bf16[128,8,384]{2,0,1:T(8,128)(2,1)} %bitcast.355), calls=%async_computation.4 | async-start | bytes 1572864 | tf_op jit(solution)/shard_map/all_to_all | solution.py:342
  400.1 85.0 %reduce-scatter.7.cloned.1.call-start = ((), (), s32[]{:S(2)}) async-start(), calls=%async_computation.18 | async-start | bytes 184320 | tf_op jit(solution)/shard_map/reduce_scatter | solution.py:366
  419.8 16.7 %all-to-all-start.3 = ((bf16[128,8,384]{2,0,1:T(8,128)(2,1)}), bf16[128,8,384]{2,0,1:T(8,128)(2,1)S(1)}, u32[]{:S(2)}, u32[]{:S(2)}) async-start(bf16[128,8,384]{2,0,1:T(8,128)(2,1)} %bitcast.271), calls=%async_computation.6 | async-start | bytes 1572864 | tf_op jit(solution)/shard_map/all_to_all | solution.py:344
  423.9 79.6 %reduce-scatter.9.cloned.1.call-start = ((), (), s32[]{:S(2)}) async-start(), calls=%async_computation.20 | async-start | bytes 737280 | tf_op jit(solution)/shard_map/reduce_scatter | solution.py:372
  427.7 3.4 copy-start.19
  427.7 3.4 copy-start.20
  427.8 3.4 copy-start.30
  427.8 3.4 copy-start.32
  431.3 2.3 copy-start.2
  431.4 2.2 copy-start.4
  431.4 2.2 copy-start.26
  431.4 2.2 copy-start.28
  431.4 2.2 copy-start.38
  433.7 2.7 copy-start.42
  433.7 7.1 %copy-start.6 = (bf16[1,1024,768]{2,1,0:T(8,128)(2,1)S(1)}, bf16[1,1024,768]{2,1,0:T(8,128)(2,1)}, u32[]{:S(2)}) copy-start(bf16[1,1024,768]{2,1,0:T(8,128)(2,1)} %all-gather.33.cloned.1.call-done) | copy-start | bytes 4718596
  436.5 4.3 copy-start.10
  436.5 20.1 %all-to-all-start = ((bf16[128,8,288]{0,2,1:T(8,128)(2,1)}), bf16[128,8,288]{0,2,1:T(8,128)(2,1)}, u32[]{:S(2)}, u32[]{:S(2)}) async-start(bf16[128,8,288]{0,2,1:T(8,128)(2,1)} %bitcast.21), calls=%async_computation | async-start | bytes 1179648 | tf_op jit(solution)/shard_map/all_to_all | solution.py:341
  440.7 82.5 %reduce-scatter.11.cloned.1.call-start = ((), (), s32[]{:S(2)}) async-start(), calls=%async_computation.21 | async-start | bytes 737280 | tf_op jit(solution)/shard_map/reduce_scatter | solution.py:378
  440.8 3.0 copy-start.8
  440.8 3.0 copy-start.36
  443.7 2.3 copy-start.9
  443.7 2.3 copy-start.40
  443.7 101.3 %reduce-scatter.5.cloned.1.call-start = ((), (), s32[]{:S(2)}) async-start(), calls=%async_computation.17 | async-start | bytes 552960 | tf_op jit(solution)/shard_map/reduce_scatter | solution.py:360
  446.4 13.3 %copy-start.14 = (bf16[1,128,768]{2,1,0:T(8,128)(2,1)S(1)}, bf16[1,128,768]{2,1,0:T(8,128)(2,1)}, u32[]{:S(2)}) copy-start(bf16[1,128,768]{2,1,0:T(8,128)(2,1)} %param.35) | copy-start | bytes 589828
  500.0 47.2 %copy-start.45 = (f32[24]{0:T(128)}, f32[24]{0:T(128)S(1)}, u32[]{:S(2)}) copy-start(f32[24]{0:T(128)S(1)} %dynamic-slice_convert_fusion.9) | copy-start | bytes 292
  (7 other events, 10.1 us)
Sparse Core Ops, SparseCore 0:
  10.8 62.8 all-gather.12
  76.6 52.8 all-gather.18
  132.3 62.4 all-gather.20
  197.5 62.3 all-gather.22
  262.2 24.6 all-gather.14
  289.2 25.8 all-gather.16
  317.6 26.0 all-gather.26
  346.1 25.8 all-gather.24
  373.9 25.6 all-gather.32
  401.9 25.7 all-gather.30
  429.6 26.9 all-gather.28
  459.3 18.4 reduce-scatter.6
  480.2 20.1 reduce-scatter.8
  502.6 20.5 reduce-scatter.10
  525.5 19.4 reduce-scatter.4
where the time goes:
time: 555 us; the launch traced here: 554 us
  waiting for transfers between devices  284 us (51%)
  blocking collectives  96.7 us (17%)
  matrix products  73 us (13%)
  other arithmetic  34 us (6%)
  local copies, waits for them, and re-layouts  29.4 us (5%)
  starting transfers between devices  17.6 us (3%)
  between operations  17.3 us (3%)
    unnamed x3, blocking collectives  77.5 us
    all_gather x1, waiting for transfers between devices, body(): lax.all_gather(reduce_weight, ('seq', 'fsdp'), axis=0, tiled=True)  57.1 us
    all_gather x1, waiting for transfers between devices, body(): lax.all_gather(expand_weight, ('seq', 'fsdp'), axis=1, tiled=True)  54.6 us
    all_gather x1, waiting for transfers between devices, body(): lax.all_gather(dense_weight, ('seq', 'fsdp'), axis=0, tiled=True)  50.3 us
    all_gather x1, waiting for transfers between devices, body(): value_piece = lax.all_gather(values_local, 'seq', axis=1, tiled=True)  28.2 us
    reduce_scatter x1, waiting for transfers between devices, body(): lax.psum_scatter(joint_term.astype(jnp.bfloat16), 'fsdp', scatter_dimensi...  20.1 us
    reduce_scatter x1, waiting for transfers between devices, body(): lax.psum_scatter(reduce_term.astype(jnp.bfloat16), 'fsdp', scatter_dimens...  18.1 us
    all_gather x1, waiting for transfers between devices, body(): key_piece = lax.all_gather(keys_local, 'seq', axis=1, tiled=True)  16 us
  transfers between devices with their start and end apart: 19, of which 12 were waited for; matrix products, arithmetic and copies ran while one was open for 24% of the time, Pallas kernels for 0%

commit v1 on v0

v1 whole, which is shorter than its diff:
```python
import math

import jax
import jax.numpy as jnp
from jax import lax
from jax.experimental import pallas as pl
from jax.experimental.pallas import tpu as pltpu
from jax.sharding import PartitionSpec as P

HD = 64
ROT = 16
EPS = 1e-05
MASKED = -1e30
MESH = pl.DeviceIdType.MESH
BF = jnp.bfloat16
F32 = jnp.float32


def greet(peers):
    barrier = pltpu.get_barrier_semaphore()
    for peer in peers:
        pl.semaphore_signal(barrier, inc=1, device_id=peer, device_id_type=MESH)
    pl.semaphore_wait(barrier, len(peers))


def gather_kernel(N, F, G, xg, wa, wb, vec, xg_all, wa_all, wb_all, vec_all, send, recv, local):
    s, f = lax.axis_index("seq"), lax.axis_index("fsdp")
    grp, g = s // G, s % G
    seq_peers = [(lax.rem(s + k, N), f) for k in range(1, N)]
    z_peers = [(s, lax.rem(f + k, F)) for k in range(1, F)]
    mates = [(grp * G + lax.rem(g + k, G), f) for k in range(1, G)]
    greet(seq_peers + z_peers)
    count = [0]

    def push(src, dst, peer):
        i = count[0]
        count[0] += 1
        copy = pltpu.make_async_remote_copy(
            src_ref=src, dst_ref=dst, send_sem=send.at[i], recv_sem=recv.at[i],
            device_id=peer, device_id_type=MESH,
        )
        copy.start()
        return copy

    own = [
        pltpu.make_async_copy(xg, xg_all.at[s], local.at[0]),
        pltpu.make_async_copy(wa, wa_all.at[g, f], local.at[1]),
        pltpu.make_async_copy(wb, wb_all.at[f], local.at[2]),
        pltpu.make_async_copy(vec, vec_all.at[s, f], local.at[3]),
    ]
    for copy in own:
        copy.start()
    vecs = [push(vec, vec_all.at[s, f], peer) for peer in z_peers]
    firsts = [push(wa, wa_all.at[g, f], peer) for peer in z_peers]
    rest = [push(xg, xg_all.at[s], peer) for peer in seq_peers]
    rest += [push(wb, wb_all.at[f], peer) for peer in z_peers]
    for copy in own:
        copy.wait()
    for copy in vecs:
        copy.wait()
    rest += [push(vec_all.at[s], vec_all.at[s], peer) for peer in seq_peers]
    for copy in firsts:
        copy.wait()
    rest += [push(wa_all.at[g], wa_all.at[g], peer) for peer in mates]
    for copy in rest:
        copy.wait()


def scatter_kernel(
    N, F, G, outp, tp, ga, gb, vecp, outr, tr, gar, gbr, vecr, ga_in, ga_sum, vec_in, vec_sum, send, recv
):
    s, f = lax.axis_index("seq"), lax.axis_index("fsdp")
    grp, g = s // G, s % G
    seq_index = [lax.rem(s + k, N) for k in range(1, N)]
    z_index = [lax.rem(f + k, F) for k in range(1, F)]
    mate_index = [lax.rem(g + k, G) for k in range(1, G)]
    greet([(p, f) for p in seq_index] + [(s, p) for p in z_index])
    count = [0]

    def push(src, dst, peer):
        i = count[0]
        count[0] += 1
        copy = pltpu.make_async_remote_copy(
            src_ref=src, dst_ref=dst, send_sem=send.at[i], recv_sem=recv.at[i],
            device_id=peer, device_id_type=MESH,
        )
        copy.start()
        return copy

    vecs = [push(vecp.at[p], vec_in.at[k], (p, f)) for k, p in enumerate(seq_index)]
    mates = [push(ga.at[p], ga_in.at[k], (grp * G + p, f)) for k, p in enumerate(mate_index)]
    rest = [push(gb.at[p], gbr.at[f], (s, p)) for p in z_index]
    for p in seq_index:
        rest.append(push(outp.at[p], outr.at[s], (p, f)))
        rest.append(push(tp.at[p], tr.at[s], (p, f)))
    outr[s] = outp[s]
    tr[s] = tp[s]
    gbr[f] = gb[f]
    for copy in vecs:
        copy.wait()
    total = vecp[s]
    for k in range(N - 1):
        total = total + vec_in[k]
    vec_sum[...] = total
    rest += [push(vec_sum.at[p], vecr.at[f], (s, p)) for p in z_index]
    vecr[f] = vec_sum[f]
    for copy in mates:
        copy.wait()
    for i in range(F):
        part = ga[g, i].astype(F32)
        for k in range(G - 1):
            part = part + ga_in[k, i].astype(F32)
        ga_sum[i] = part.astype(BF)
    rest += [push(ga_sum.at[p], gar.at[f], (s, p)) for p in z_index]
    gar[f] = ga_sum[f]
    for copy in rest:
        copy.wait()


def gather_phase(N, F, G, xg, wa, wb, vec):
    copies = 3 * (F - 1) + 2 * (N - 1) + G - 1
    hbm = pl.BlockSpec(memory_space=pl.ANY)
    return pl.pallas_call(
        lambda *refs: gather_kernel(N, F, G, *refs),
        out_shape=(
            jax.ShapeDtypeStruct((N,) + xg.shape, xg.dtype),
            jax.ShapeDtypeStruct((G, F) + wa.shape, wa.dtype),
            jax.ShapeDtypeStruct((F,) + wb.shape, wb.dtype),
            jax.ShapeDtypeStruct((N, F) + vec.shape, vec.dtype),
        ),
        in_specs=[hbm] * 4,
        out_specs=(hbm,) * 4,
        scratch_shapes=[
            pltpu.SemaphoreType.DMA((copies,)),
            pltpu.SemaphoreType.DMA((copies,)),
            pltpu.SemaphoreType.DMA((4,)),
        ],
        compiler_params=pltpu.CompilerParams(collective_id=0, has_side_effects=True),
    )(xg, wa, wb, vec)


def scatter_phase(N, F, G, outp, tp, ga, gb, vecp):
    copies = 3 * (F - 1) + 3 * (N - 1) + G - 1
    vmem = pl.BlockSpec(memory_space=pltpu.VMEM)
    return pl.pallas_call(
        lambda *refs: scatter_kernel(N, F, G, *refs),
        out_shape=(
            jax.ShapeDtypeStruct(outp.shape, BF),
            jax.ShapeDtypeStruct(tp.shape, BF),
            jax.ShapeDtypeStruct(ga.shape[1:], BF),
            jax.ShapeDtypeStruct(gb.shape, BF),
            jax.ShapeDtypeStruct(vecp.shape[1:], F32),
        ),
        in_specs=[vmem] * 5,
        out_specs=(vmem,) * 5,
        scratch_shapes=[
            pltpu.VMEM((max(G - 1, 1),) + ga.shape[1:], BF),
            pltpu.VMEM(ga.shape[1:], BF),
            pltpu.VMEM((N - 1,) + vecp.shape[1:], F32),
            pltpu.VMEM(vecp.shape[1:], F32),
            pltpu.SemaphoreType.DMA((copies,)),
            pltpu.SemaphoreType.DMA((copies,)),
        ],
        compiler_params=pltpu.CompilerParams(
            collective_id=1, has_side_effects=True, vmem_limit_bytes=48 * 2**20
        ),
    )(outp, tp, ga, gb, vecp)


def row_places(pair_held, count, block_rows):
    pair_count = pair_held.shape[0]
    blocks = jnp.stack([pair_held, 2 * pair_count - 1 - pair_held], axis=1).reshape(-1)
    inside = jnp.arange(block_rows, dtype=jnp.int32)
    return (blocks[:, None] * block_rows + inside[None, :]).reshape(count)


def turn(values, cosine, sine):
    half = ROT // 2
    low, high = values[..., :half], values[..., half:ROT]
    return jnp.concatenate(
        [low * cosine - high * sine, high * cosine + low * sine, values[..., ROT:]], axis=-1
    )


def nt(left, right):
    return lax.dot_general(left, right, (((1,), (1,)), ((), ())), preferred_element_type=F32)


def nn(left, right):
    return jnp.dot(left, right, preferred_element_type=F32)


def tn(left, right):
    return lax.dot_general(left, right, (((0,), (0,)), ((), ())), preferred_element_type=F32)


def pad_rows(array, axis, multiple=16):
    extra = -array.shape[axis] % multiple
    if extra == 0:
        return array
    widths = [(0, 0)] * array.ndim
    widths[axis] = (0, extra)
    return jnp.pad(array, widths)


def make_body(N, F):
    def body(
        tokens, pair_held, joint_weight, joint_bias, dense_weight, dense_bias, expand_weight,
        expand_bias, reduce_weight, reduce_bias, first_gain, first_shift, second_gain,
        second_shift, cotangent,
    ):
        _, R, D = tokens.shape
        L = N * R
        H = D // HD
        G = N // math.gcd(N, H)
        HG = H * G // N
        W = HG * HD
        Q = L // G
        cj, cd, ce = joint_weight.shape[1], dense_weight.shape[0], expand_weight.shape[1]
        s = lax.axis_index("seq")
        grp, gi = s // G, s % G
        scale = HD ** (-0.5)

        xg = jnp.concatenate([tokens, cotangent], axis=0)
        wa = pad_rows(jnp.concatenate([joint_weight.T, dense_weight], axis=0), 0)
        wb = pad_rows(jnp.concatenate([expand_weight.T, reduce_weight], axis=0), 0)
        vec = jnp.concatenate(
            [first_gain, first_shift, second_gain, second_shift, joint_bias, dense_bias,
             expand_bias, reduce_bias]
        ).astype(F32)
        vec = jnp.pad(vec, (0, 1024 - vec.shape[0])).reshape(8, 128)
        xg_all, wa_all, wb_all, vec_all = gather_phase(N, F, G, xg, wa, wb, vec)

        va = vec_all.reshape(N * F, 1024)
        gain1, shift1, gain2, shift2 = [
            va[:, i * cd:(i + 1) * cd].reshape(D) for i in range(4)
        ]
        at = 4 * cd
        bias_j = lax.dynamic_slice_in_dim(va[:, at:at + cj], grp * G * F, G * F, 0).reshape(HG, 3, HD)
        at += cj
        bias_d = va[:, at:at + cd].reshape(D)
        at += cd
        bias_e = lax.dynamic_slice_in_dim(va[:, at:at + ce], s * F, F, 0).reshape(F * ce)
        at += ce
        bias_r = va[:, at:at + cd].reshape(D)

        joint = wa_all[:, :, :cj].reshape(HG, 3, HD, D)
        wq, wk, wv = [joint[:, i].reshape(W, D) for i in range(3)]
        dense = wa_all[:, :, cj:cj + cd].reshape(W, D)
        expand = wb_all[:, :ce].reshape(F * ce, D)
        reduce_w = wb_all[:, ce:2 * ce].reshape(F * ce, D)

        x = xg_all[:, 0].reshape(L, D).astype(F32)
        grad = xg_all[:, 1].reshape(L, D)
        center = x - jnp.mean(x, axis=-1, keepdims=True)
        inv = lax.rsqrt(jnp.mean(center * center, axis=-1, keepdims=True) + EPS)
        n = center * inv
        nf1 = (n * gain1 + shift1).astype(BF)
        nf2 = (n * gain2 + shift2).astype(BF)

        def mine(array):
            return lax.dynamic_slice_in_dim(array, gi * Q, Q, 0)

        def own_rows(array):
            pick = (jnp.arange(G) == gi)[:, None, None]
            return jnp.where(pick, array[None], 0.0).reshape(L, D)

        places = row_places(pair_held, L, R // 2)
        freq = 1.0 / 10000.0 ** (jnp.arange(0, ROT, 2, dtype=F32) / ROT)
        angles = places.astype(F32)[:, None] * freq[None, :]
        cosine, sine = jnp.cos(angles)[:, None], jnp.sin(angles)[:, None]
        cos_q, sin_q, places_q = mine(cosine), mine(sine), mine(places)

        nf1_q, grad_q = mine(nf1), mine(grad)
        q = turn(nt(nf1_q, wq).reshape(Q, HG, HD) + bias_j[:, 0], cos_q, sin_q).astype(BF)
        k = turn(nt(nf1, wk).reshape(L, HG, HD) + bias_j[:, 1], cosine, sine).astype(BF)
        v = (nt(nf1, wv).reshape(L, HG, HD) + bias_j[:, 2]).astype(BF)
        gctx = nt(grad_q, dense).astype(BF).reshape(Q, HG, HD)

        allowed = places_q[:, None] >= places[None, :]
        scores = jnp.einsum("qhd,khd->hqk", q, k, preferred_element_type=F32) * scale
        scores = jnp.where(allowed, scores, MASKED)
        peak = jnp.max(scores, axis=-1, keepdims=True)
        weight = jnp.exp(scores - peak)
        probs_full = weight / jnp.sum(weight, axis=-1, keepdims=True)
        probs = probs_full.astype(BF)
        context = jnp.einsum("hqk,khd->qhd", probs, v, preferred_element_type=F32)
        ctx_low = context.reshape(Q, W).astype(BF)
        g_probs = jnp.einsum("qhd,khd->hqk", gctx, v, preferred_element_type=F32)
        delta = jnp.sum(probs_full * g_probs, axis=-1, keepdims=True)
        g_scores = (probs_full * (g_probs - delta)).astype(BF)
        gq = jnp.einsum("hqk,khd->qhd", g_scores, k, preferred_element_type=F32) * scale
        gk = jnp.einsum("hqk,qhd->khd", g_scores, q, preferred_element_type=F32) * scale
        gv = jnp.einsum("hqk,qhd->khd", probs, gctx, preferred_element_type=F32)
        gq = turn(gq, cos_q, -sin_q).astype(BF).reshape(Q, W)
        gk = turn(gk, cosine, -sine).astype(BF).reshape(L, W)
        gv = gv.astype(BF).reshape(L, W)

        hidden = nt(nf2, expand) + bias_e
        active, gelu_pull = jax.vjp(lambda t: jax.nn.gelu(t, approximate=False), hidden)
        active = active.astype(BF)
        out_part = nn(active, reduce_w) + own_rows(nn(ctx_low, dense))
        g_hidden = gelu_pull(nt(grad, reduce_w))[0].astype(BF)
        g2 = nn(g_hidden, expand)
        g1 = nn(gk, wk) + nn(gv, wv) + own_rows(nn(gq, wq))
        t_part = g1 * gain1 + g2 * gain2

        d_joint = jnp.stack(
            [tn(gq, nf1_q).astype(BF).reshape(HG, HD, D), tn(gk, nf1).astype(BF).reshape(HG, HD, D),
             tn(gv, nf1).astype(BF).reshape(HG, HD, D)], axis=1
        ).reshape(G, F, cj, D)
        d_dense = tn(ctx_low, grad_q).astype(BF).reshape(G, F, cd, D)
        ga = pad_rows(jnp.concatenate([d_joint, d_dense], axis=2), 2)
        gb = pad_rows(
            jnp.concatenate(
                [tn(g_hidden, nf2).astype(BF).reshape(F, ce, D),
                 tn(active, grad).astype(BF).reshape(F, ce, D)], axis=1), 1
        )

        def col(array):
            return jnp.sum(array.astype(F32), axis=0)

        owner_s = jnp.arange(N * F) // F
        gains = [
            p.reshape(N * F, cd)
            for p in (jnp.sum(g1 * n, axis=0), jnp.sum(g1, axis=0), jnp.sum(g2 * n, axis=0), jnp.sum(g2, axis=0))
        ]
        b_joint = jnp.stack([col(a).reshape(HG, HD) for a in (gq, gk, gv)], axis=1).reshape(G * F, cj)
        b_joint = lax.dynamic_update_slice_in_dim(jnp.zeros((N * F, cj), F32), b_joint, grp * G * F, 0)
        b_expand = lax.dynamic_update_slice_in_dim(
            jnp.zeros((N * F, ce), F32), col(g_hidden).reshape(F, ce), s * F, 0
        )
        b_out = jnp.where((owner_s == s)[:, None], col(grad).reshape(N * F, cd), 0.0)
        vecp = jnp.concatenate(gains + [b_joint, b_out, b_expand], axis=1)
        vecp = jnp.pad(vecp, ((0, 0), (0, 1024 - vecp.shape[1]))).reshape(N, F, 8, 128)

        outr, tr, gar, gbr, vecr = scatter_phase(
            N, F, G, out_part.astype(BF).reshape(N, R, D), t_part.astype(BF).reshape(N, R, D),
            ga, gb, vecp
        )
        x_own = tokens[0].astype(F32)
        layer_output = (x_own + jnp.sum(outr.astype(F32), axis=0) + bias_d + bias_r).astype(BF)
        center = x_own - jnp.mean(x_own, axis=-1, keepdims=True)
        inv_own = lax.rsqrt(jnp.mean(center * center, axis=-1, keepdims=True) + EPS)
        n_own = center * inv_own
        t = jnp.sum(tr.astype(F32), axis=0)
        g_in = (
            t - jnp.mean(t, axis=-1, keepdims=True)
            - n_own * jnp.mean(t * n_own, axis=-1, keepdims=True)
        ) * inv_own
        input_grad = (cotangent[0].astype(F32) + g_in).astype(BF)
        a = jnp.sum(gar.astype(F32), axis=0)
        b = jnp.sum(gbr.astype(F32), axis=0)
        vs = jnp.sum(vecr, axis=0).reshape(1024)
        at = 4 * cd
        o_joint, at = vs[at:at + cj], at + cj
        o_out, at = vs[at:at + cd], at + cd
        o_expand = vs[at:at + ce]
        return (
            layer_output[None], input_grad[None], a[:cj].T, o_joint, a[cj:cj + cd], o_out,
            b[:ce].T, o_expand, b[ce:2 * ce], o_out,
            vs[:cd], vs[cd:2 * cd], vs[2 * cd:3 * cd], vs[3 * cd:4 * cd],
        )

    return body


def solution(mesh):
    both = ("seq", "fsdp")
    cols, rows, vector = P(None, both), P(both, None), P(both)
    acts = P("fsdp", "seq", None)
    return jax.shard_map(
        make_body(mesh.shape["seq"], mesh.shape["fsdp"]),
        mesh=mesh,
        in_specs=(
            acts, P(), cols, vector, rows, vector, cols, vector, rows, vector,
            vector, vector, vector, vector, acts,
        ),
        out_specs=(
            acts, acts, cols, vector, rows, vector, cols, vector, rows, vector,
            vector, vector, vector, vector,
        ),
        check_vma=False,
    )
```

time: 555 us -> 183 us (0.33)
  waiting for transfers between devices: 284 us -> 0 us
  blocking collectives: 96.7 us -> 0 us
  Pallas kernels: 0 us -> 89.1 us
  matrix products: 73 us -> 38.9 us
  starting transfers between devices: 17.6 us -> 0 us
  between operations: 17.3 us -> 1.78 us
  other arithmetic: 34 us -> 26.3 us
    all_gather x11 -> x0, waiting for transfers between devices: 241 us -> none  [the longest x1 57.1 us: body(): lax.all_gather(reduce_weight, ('seq', 'fsdp'), axis=0, tiled=True)]
    pallas_call x0 -> x2, Pallas kernels: none -> 89.1 us  [the longest x1 45.8 us: scatter_phase(): pl.pallas_call(lambda *refs: scatter_kernel(N, F, G, *refs), out_shape=(j...]
    unnamed x3 -> x0, blocking collectives: 77.5 us -> none
    dot_general x26 -> x23, matrix products: 73 us -> 33.9 us  [the longest x6 11.3 us: nt(): lax.dot_general(left, right, (((1,), (1,)), ((), ())), preferred_element_...]
    reduce_scatter x4 -> x0, waiting for transfers between devices: 38.3 us -> none  [the longest x1 20.1 us: body(): lax.psum_scatter(joint_term.astype(jnp.bfloat16), 'fsdp', scatter_dimensi...]
    all_gather x2 -> x0, blocking collectives: 19.2 us -> none  [the longest x1 10.1 us: body(): lax.all_gather(row_delta, 'seq', axis=2, tiled=True)]
    all_to_all x4 -> x0, starting transfers between devices: 16.9 us -> none  [the longest x1 4.35 us: body(): lax.all_to_all(g_hidden, 'seq', split_axis=1, concat_axis=0, tiled=True)]
    convert_element_type x24 -> x5, other arithmetic: 15.4 us -> 4.27 us  [the longest x1 1.28 us: body(): g_scores = (probs_full * (g_probs - delta)).astype(BF)]
  transfers between devices with their start and end apart: 19 -> 0, of which waited for: 12 -> 0; matrix products, arithmetic and copies ran while one was open for 24% -> 0% of each run, Pallas kernels for 0% -> 0%
where the time goes in v1:
time: 183 us
  Pallas kernels  89.1 us (49%)
  matrix products  38.9 us (21%)
  local copies, waits for them, and re-layouts  26.6 us (15%)
  other arithmetic  26.3 us (14%)
    pallas_call x1, Pallas kernels, scatter_phase(): pl.pallas_call(lambda *refs: scatter_kernel(N, F, G, *refs), out_shape=(j...  45.8 us
    pallas_call x1, Pallas kernels, gather_phase(): pl.pallas_call(lambda *refs: gather_kernel(N, F, G, *refs), out_shape=(ja...  43.3 us
    unnamed x142, local copies, waits for them, and re-layouts  11.5 us
    dot_general x6, matrix products, nt(): lax.dot_general(left, right, (((1,), (1,)), ((), ())), preferred_element_...  11.3 us
    dot_general x6, matrix products, nn(): return jnp.dot(left, right, preferred_element_type=F32)  9.14 us
    concatenate x1, local copies, waits for them, and re-layouts, body(): jnp.concatenate([first_gain, first_shift, second_gain, second_shift, join...  5.44 us
    dot_general x6, matrix products, tn(): lax.dot_general(left, right, (((0,), (0,)), ((), ())), preferred_element_...  4.97 us
    sub x1, matrix products, body(): weight = jnp.exp(scores - peak)  4.95 us

profile of v1, /device:TPU:0, one launch (start us, length us, event | category | flops | bytes accessed | tf_op | source)
XLA Modules:
  0.0 182.6 jit_solution(3265494188974198784)
XLA Ops:
  0.7 0.8 subtract_bitcast_fusion
  1.5 0.7 add_multiply_fusion
  2.2 1.0 convert_reduce_fusion.10
  3.7 1.1 fusion.51
  5.4 5.4 %concatenate.39 = bf16[312]{0:T(512)(128)(2,1)S(1)} concatenate(bf16[24]{0:T(256)(128)(2,1)} %param.25, bf16[24]{0:T(256)(128)(2,1)} %param.26, bf16[24]{0:T(256)(128)(2,1)} %param.27, bf16[24]{0:T(256)(128)(2,1)} %param.28, bf16[72]{0:T(256)(128)(2,1)} %param.18, bf16[24]{0:T(256)(128)(2,1)} %param.20, bf16[96]{0:T(256)(128)(2,1)} %param.22, bf16[24]{0:T(256)(128)(2,1)} %param.24), dimensions={0} | concatenate | bytes 1248 | tf_op jit(solution)/shard_map/concatenate | solution.py:227
  10.9 0.6 broadcast_in_dim.86
  11.4 0.6 bitcast_convert_fusion.refs_3_
  12.4 0.8 fusion.59
  13.2 0.6 fusion.73
  13.9 1.6 pad_maximum_fusion.8.refs_1_
  15.5 1.7 pad_maximum_fusion.6.refs_2_
  17.2 0.8 pad_maximum_fusion.3.refs_0_
  18.0 1.2 broadcast_compare_fusion
  19.1 43.3 %shard_map.254 = (bf16[8,2,128,768]{3,2,1,0:T(8,128)(2,1)}, bf16[2,4,96,768]{3,2,1,0:T(8,128)(2,1)}, bf16[4,192,768]{2,1,0:T(8,128)(2,1)}, f32[8,4,8,128]{3,2,1,0:T(8,128)}) custom-call(bf16[2,128,768]{2,1,0:T(8,128)(2,1)} %pad_maximum_fusion.3.refs_0_, bf16[96,768]{1,0:T(8,128)(2,1)} %pad_maximum_fusion.8.refs_1_, ...), custom_call_target="tpu_custom_call" | custom-call | tf_op jit(solution)/shard_map/pallas_call | solution.py:123
  62.5 0.9 copy.55
  63.4 1.7 convert_reduce_fusion.4
  65.1 0.6 fusion.67
  65.7 2.8 %convert_reduce_fusion.3 = (f32[768]{0:T(1024)S(1)}, f32[8,128]{1,0:T(8,128)S(1)}) fusion(bf16[8,2,128,768]{3,2,1,0:T(8,128)(2,1)} %get-tuple-element.23, f32[8,128]{1,0:T(8,128)S(1)} %get-tuple-element.87), kind=kLoop, calls=%fused_computation.16 | loop fusion | flops 4716800 | bytes 3156992 | tf_op jit(solution)/shard_map/reduce_sum | solution.py:321
  68.4 0.6 fusion.68
  69.1 0.7 broadcast_select_fusion
  70.1 0.7 add.246
  71.8 0.7 add.249
  72.6 0.9 fusion.75
  73.6 0.9 copy-done.23
  74.6 0.9 copy-done.2
  75.6 1.2 convolution_convert_fusion.5
  76.8 0.9 add_convert_fusion.2
  77.7 1.0 convolution_add_fusion
  78.7 1.4 fusion.26
  80.1 0.7 convolution_add_fusion.1
  80.8 0.7 subtract_convert_fusion.1
  81.5 0.8 slice.249
  82.2 5.3 %convert_reduce_fusion.6 = (f32[384]{0:T(512)S(1)}, bf16[1024,384]{1,0:T(8,128)(2,1)}, f32[1024,384]{1,0:T(8,128)S(1)}) fusion(f32[1024,384]{1,0:T(8,128)S(1)} %convolution_add_fusion, bf16[1024,768]{1,0:T(8,128)(2,1)S(1)} %bitcast.169, bf16[384,768]{1,0:T(8,128)(2,1)S(1)} %bitcast.186), kind=kOutput, calls=%fused_computation.36 | convolution fusion | flops 633077376 | bytes 6096384 | tf_op jit(solution)/shard_map/dot_general | solution.py:186
  87.5 1.2 multiply_convert_fusion.1
  88.8 2.5 %convolution_convert_fusion = bf16[384,768]{1,0:T(8,128)(2,1)S(1)} fusion(bf16[1024,384]{1,0:T(8,128)(2,1)} %multiply_convert_fusion.1, bf16[1024,768]{1,0:T(8,128)(2,1)} %bitcast.170), kind=kOutput, calls=%fused_computation.60 | convolution fusion | flops 604274688 | bytes 2949120 | tf_op jit(solution)/shard_map/dot_general | solution.py:194
  92.0 1.8 convolution_add_fusion.3
  94.1 0.8 fusion.24
  95.1 0.8 copy-done.24
  96.1 5.0 %fusion.80 = (f32[3,512]{1,0:T(4,128)S(1)}, f32[3,512,1024]{2,1,0:T(8,128)}) fusion(pred[512,1024]{1,0:T(8,128)(4,1)S(1)} %copy-done.29, bf16[512,3,48]{0,2,1:T(8,128)(2,1)S(1)} %slice.250, bf16[512,3,8]{0,2,1:T(8,128)(2,1)S(1)} %get-tuple-element.66, bf16[512,3,8]{0,2,1:T(8,128)(2,1)S(1)} %get-tuple-element.65, bf16[1024,3,48]{0,2,1:T(8,128)(2,1)S(1)} %copy-done.24, ...), kind=kOutput, calls=%fused_computation.182 | convolution fusion | flops 209388544 | bytes 7411712 | tf_op jit(solution)/shard_map/sub | solution.py:284
  101.1 4.1 %fusion.31 = bf16[3,64,512]{2,1,0:T(8,128)(2,1)S(1)} fusion(bf16[1024,3,64]{0,2,1:T(8,128)(2,1)S(1)} %copy-done.66, f32[3,512,1024]{2,1,0:T(8,128)} %get-tuple-element.91, f32[3,512]{1,0:T(4,128)S(1)} %get-tuple-element.90), kind=kOutput, calls=%fused_computation.77 | convolution fusion | flops 204570624 | bytes 6887424 | tf_op jit(solution)/shard_map/hqk,khd->qhd/dot_general | solution.py:287
  105.5 0.6 copy-done.11
  106.1 0.9 convert_reduce_fusion.8
  108.5 0.7 copy-done.10
  109.4 2.2 %fusion.4 = bf16[1024,768]{1,0:T(8,128)(2,1)} fusion(bf16[1024,384]{1,0:T(8,128)(2,1)S(1)} %copy-done.10, bf16[384,768]{1,0:T(8,128)(2,1)S(1)} %bitcast.187, f32[512,768]{1,0:T(8,128)S(1)} %fusion.81, pred[1024]{0:T(1024)(128)(4,1)S(1)} %copy-done.55), kind=kOutput, calls=%fused_computation.12 | convolution fusion | flops 606339072 | bytes 4523008 | tf_op jit(solution)/shard_map/dot_general | solution.py:190
  111.5 1.8 multiply_reduce_fusion
  113.3 1.3 multiply_convert_fusion
  114.6 1.1 fusion.30
  115.7 0.7 fusion.25
  116.6 1.0 copy-done.9
  119.3 1.4 fusion.83
  120.7 1.6 fusion.82
  122.4 0.7 fusion.2
  123.2 1.1 copy-done.3
  124.6 2.8 %multiply_reduce_fusion.1 = (f32[768]{0:T(1024)S(1)}, f32[768]{0:T(1024)S(1)}, f32[768]{0:T(1024)S(1)}, f32[768]{0:T(1024)S(1)}, bf16[1024,768]{1,0:T(8,128)(2,1)}) fusion(f32[1024]{0:T(1024)S(1)} %copy-done.49, f32[1024]{0:T(1024)S(1)} %copy-done.47, bf16[8,2,128,768]{3,2,1,0:T(8,128)(2,1)S(1)} %copy-done.3, f32[1024,768]{1,0:T(8,128)S(1)} %fusion.2, ...), kind=kOutput, calls=%fused_computation.17 | convolution fusion | flops 614200320 | bytes 7694336 | tf_op jit(solution)/shard_map/dot_general | solution.py:190
  127.9 45.8 %shard_map.255 = (bf16[8,128,768]{2,1,0:T(8,128)(2,1)S(1)}, bf16[8,128,768]{2,1,0:T(8,128)(2,1)}, bf16[4,96,768]{2,1,0:T(8,128)(2,1)S(1)}, bf16[4,192,768]{2,1,0:T(8,128)(2,1)S(1)}, f32[4,8,128]{2,1,0:T(8,128)S(1)}) custom-call(bf16[8,128,768]{2,1,0:T(8,128)(2,1)} %bitcast.176, bf16[8,128,768]{2,1,0:T(8,128)(2,1)} %bitcast.193, ...), custom_call_target="tpu_custom_call" | custom-call | tf_op jit(solution)/shard_map/pallas_call | solution.py:145
  173.7 0.8 copy-done
  174.8 0.6 slice.169
  175.4 0.6 slice.165
  176.0 0.6 fusion.79
  176.7 0.6 slice.202
  177.4 0.7 slice_bitcast_fusion.1
  178.1 1.8 %convert_reduce_fusion = (f32[128]{0:T(128)S(1)}, f32[128,768]{1,0:T(8,128)S(1)}) fusion(bf16[8,128,768]{2,1,0:T(8,128)(2,1)} %get-tuple-element.28), kind=kLoop, calls=%fused_computation.6 | loop fusion | flops 2260864 | bytes 1966592 | tf_op jit(solution)/shard_map/reduce_sum | solution.py:348
  180.2 0.9 fusion.47
  181.3 0.8 fusion.76
  (201 shorter events, 10.3 us)
Async XLA Ops:
  0.6 16.5 %copy-start.12 = (bf16[1,128,768]{2,1,0:T(8,128)(2,1)S(1)}, bf16[1,128,768]{2,1,0:T(8,128)(2,1)}, u32[]{:S(2)}) copy-start(bf16[1,128,768]{2,1,0:T(8,128)(2,1)} %param.15) | copy-start | bytes 589828
  0.7 16.5 %copy-start.25 = (bf16[1,128,768]{2,1,0:T(8,128)(2,1)S(1)}, bf16[1,128,768]{2,1,0:T(8,128)(2,1)}, u32[]{:S(2)}) copy-start(bf16[1,128,768]{2,1,0:T(8,128)(2,1)} %param.29) | copy-start | bytes 589828
  65.7 6.9 %copy-start.22 = (bf16[2,4,96,768]{3,2,1,0:T(8,128)(2,1)S(1)}, bf16[2,4,96,768]{3,2,1,0:T(8,128)(2,1)}, u32[]{:S(2)}) copy-start(bf16[2,4,96,768]{3,2,1,0:T(8,128)(2,1)} %get-tuple-element.26) | copy-start | bytes 3538948
  71.5 5.2 %copy-start.34 = (f32[768]{0:T(1024)}, f32[768]{0:T(1024)S(1)}, u32[]{:S(2)}) copy-start(f32[768]{0:T(1024)S(1)} %mul.338) | copy-start | bytes 9220
  71.6 5.1 %copy-start.37 = (f32[768]{0:T(1024)}, f32[768]{0:T(1024)S(1)}, u32[]{:S(2)}) copy-start(f32[768]{0:T(1024)S(1)} %add.215) | copy-start | bytes 9220
  71.7 5.0 %copy-start.50 = (f32[768]{0:T(1024)}, f32[768]{0:T(1024)S(1)}, u32[]{:S(2)}) copy-start(f32[768]{0:T(1024)S(1)} %mul.331) | copy-start | bytes 9220
  71.8 4.9 %copy-start.53 = (f32[768]{0:T(1024)}, f32[768]{0:T(1024)S(1)}, u32[]{:S(2)}) copy-start(f32[768]{0:T(1024)S(1)} %add.207) | copy-start | bytes 9220
  72.6 1.9 %copy-start.23 = (bf16[4,192,768]{2,1,0:T(8,128)(2,1)S(1)}, bf16[4,192,768]{2,1,0:T(8,128)(2,1)}, u32[]{:S(2)}) copy-start(bf16[4,192,768]{2,1,0:T(8,128)(2,1)} %get-tuple-element.25) | copy-start | bytes 3538948
  72.6 7.5 %copy-start.14 = (bf16[2,4,72,768]{3,2,1,0:T(8,128)(2,1)}, bf16[2,4,72,768]{3,2,1,0:T(8,128)(2,1)S(1)}, u32[]{:S(2)}) copy-start(bf16[2,4,72,768]{3,2,1,0:T(8,128)(2,1)S(1)} %slice.140) | copy-start | bytes 2654212
  72.6 2.8 %copy-start.2 = (bf16[8,2,128,768]{3,2,1,0:T(8,128)(2,1)S(1)}, bf16[8,2,128,768]{3,2,1,0:T(8,128)(2,1)}, u32[]{:S(2)}) copy-start(bf16[8,2,128,768]{3,2,1,0:T(8,128)(2,1)} %get-tuple-element.23) | copy-start | bytes 9437188
  74.5 3.1 %copy-start.27 = (bf16[4,96,768]{2,1,0:T(8,128)(2,1)}, bf16[4,96,768]{2,1,0:T(8,128)(2,1)S(1)}, u32[]{:S(2)}) copy-start(bf16[4,96,768]{2,1,0:T(8,128)(2,1)S(1)} %get-tuple-element.52) | copy-start | bytes 1769476
  74.6 7.7 %copy-start.17 = (bf16[4,96,768]{2,1,0:T(8,128)(2,1)}, bf16[4,96,768]{2,1,0:T(8,128)(2,1)S(1)}, u32[]{:S(2)}) copy-start(bf16[4,96,768]{2,1,0:T(8,128)(2,1)S(1)} %get-tuple-element.53) | copy-start | bytes 1769476
  75.5 6.7 %copy-start.4 = (bf16[8,1,128,768]{3,2,1,0:T(8,128)(2,1)}, bf16[8,1,128,768]{3,2,1,0:T(8,128)(2,1)S(1)}, u32[]{:S(2)}) copy-start(bf16[8,1,128,768]{3,2,1,0:T(8,128)(2,1)S(1)} %slice.155) | copy-start | bytes 4718596
  77.7 2.5 %copy-start.6 = (bf16[8,1,128,768]{3,2,1,0:T(8,128)(2,1)}, bf16[8,1,128,768]{3,2,1,0:T(8,128)(2,1)S(1)}, u32[]{:S(2)}) copy-start(bf16[8,1,128,768]{3,2,1,0:T(8,128)(2,1)S(1)} %get-tuple-element.50) | copy-start | bytes 4718596
  88.6 2.6 %copy-start.46 = (f32[1024]{0:T(1024)S(1)}, f32[1024]{0:T(1024)}, u32[]{:S(2)}) copy-start(f32[1024]{0:T(1024)} %get-tuple-element.86) | copy-start | bytes 12292
  88.7 2.6 %copy-start.48 = (f32[1024]{0:T(1024)S(1)}, f32[1024]{0:T(1024)}, u32[]{:S(2)}) copy-start(f32[1024]{0:T(1024)} %get-tuple-element.88) | copy-start | bytes 12292
  88.7 2.5 %copy-start.40 = (f32[32,96]{1,0:T(8,128)}, f32[32,96]{1,0:T(8,128)S(1)}, u32[]{:S(2)}) copy-start(f32[32,96]{1,0:T(8,128)S(1)} %constant_dynamic-update-slice_fusion) | copy-start | bytes 36868
  91.9 3.0 %copy-start.8 = (f32[1024,768]{1,0:T(8,128)}, f32[1024,768]{1,0:T(8,128)S(1)}, u32[]{:S(2)}) copy-start(f32[1024,768]{1,0:T(8,128)S(1)} %fusion.5) | copy-start | bytes 9437188
  92.0 1.8 copy-start.32
  92.0 1.8 copy-start.43
  92.0 1.9 %copy-start.51 = (f32[768]{0:T(1024)S(1)}, f32[768]{0:T(1024)}, u32[]{:S(2)}) copy-start(f32[768]{0:T(1024)} %copy-done.50) | copy-start | bytes 9220
  92.0 1.9 %copy-start.54 = (f32[768]{0:T(1024)S(1)}, f32[768]{0:T(1024)}, u32[]{:S(2)}) copy-start(f32[768]{0:T(1024)} %copy-done.53) | copy-start | bytes 9220
  92.0 2.1 %copy-start.64 = (bf16[1024,384]{1,0:T(8,128)(2,1)S(1)}, bf16[1024,384]{1,0:T(8,128)(2,1)}, u32[]{:S(2)}) copy-start(bf16[1024,384]{1,0:T(8,128)(2,1)} %get-tuple-element.41) | copy-start | bytes 2359300
  94.9 1.0 copy-start.24
  95.0 1.1 copy-start.29
  95.0 1.1 copy-start.30
  96.1 5.0 %copy-start.66 = (bf16[1024,3,64]{0,2,1:T(8,128)(2,1)S(1)}, bf16[1024,3,64]{0,2,1:T(8,128)(2,1)}, u32[]{:S(2)}) copy-start(bf16[1024,3,64]{0,2,1:T(8,128)(2,1)} %fusion.26) | copy-start | bytes 1179652
  101.0 4.5 %copy-start.57 = (f32[3,512]{1,0:T(4,128)}, f32[3,512]{1,0:T(4,128)S(1)}, u32[]{:S(2)}) copy-start(f32[3,512]{1,0:T(4,128)S(1)} %get-tuple-element.90) | copy-start | bytes 18436
  101.0 4.1 %copy-start.5 = (bf16[8,1,128,768]{3,2,1,0:T(8,128)(2,1)S(1)}, bf16[8,1,128,768]{3,2,1,0:T(8,128)(2,1)}, u32[]{:S(2)}) copy-start(bf16[8,1,128,768]{3,2,1,0:T(8,128)(2,1)} %copy-done.4) | copy-start | bytes 4718596
  101.0 5.1 %copy-start.11 = (f32[3,512,1024]{2,1,0:T(8,128)S(1)}, f32[3,512,1024]{2,1,0:T(8,128)}, u32[]{:S(2)}) copy-start(f32[3,512,1024]{2,1,0:T(8,128)} %get-tuple-element.91) | copy-start | bytes 18874372
  101.1 5.1 %copy-start.31 = (bf16[512,192]{0,1:T(8,128)(2,1)S(1)}, bf16[512,192]{0,1:T(8,128)(2,1)}, u32[]{:S(2)}) copy-start(bf16[512,192]{0,1:T(8,128)(2,1)} %convolution_convert_fusion.5) | copy-start | bytes 589828
  106.1 1.4 copy-start.7
  107.0 1.5 copy-start.19
  108.1 1.1 copy-start.10
  108.1 1.3 copy-start.18
  108.1 1.3 copy-start.55
  109.4 2.2 %copy-start.58 = (f32[3,512]{1,0:T(4,128)S(1)}, f32[3,512]{1,0:T(4,128)}, u32[]{:S(2)}) copy-start(f32[3,512]{1,0:T(4,128)} %copy-done.57) | copy-start | bytes 18436
  109.4 2.2 %copy-start.67 = (bf16[1024,3,64]{0,2,1:T(8,128)(2,1)S(1)}, bf16[1024,3,64]{0,2,1:T(8,128)(2,1)}, u32[]{:S(2)}) copy-start(bf16[1024,3,64]{0,2,1:T(8,128)(2,1)} %fusion.26) | copy-start | bytes 1179652
  115.7 0.7 copy-start.42
  115.7 1.9 %copy-start.9 = (f32[1024,768]{1,0:T(8,128)S(1)}, f32[1024,768]{1,0:T(8,128)}, u32[]{:S(2)}) copy-start(f32[1024,768]{1,0:T(8,128)} %copy-done.8) | copy-start | bytes 9437188
  116.4 1.5 copy-start.33
  118.2 0.7 copy-start.15
  119.1 1.5 copy-start.16
  120.6 1.7 copy-start.20
  120.7 1.7 copy-start.21
  120.7 1.7 copy-start.56
  122.4 1.9 %copy-start.3 = (bf16[8,2,128,768]{3,2,1,0:T(8,128)(2,1)S(1)}, bf16[8,2,128,768]{3,2,1,0:T(8,128)(2,1)}, u32[]{:S(2)}) copy-start(bf16[8,2,128,768]{3,2,1,0:T(8,128)(2,1)} %get-tuple-element.23) | copy-start | bytes 9437188
  122.4 2.0 %copy-start.28 = (bf16[4,96,768]{2,1,0:T(8,128)(2,1)S(1)}, bf16[4,96,768]{2,1,0:T(8,128)(2,1)}, u32[]{:S(2)}) copy-start(bf16[4,96,768]{2,1,0:T(8,128)(2,1)} %copy-done.27) | copy-start | bytes 1769476
  122.4 2.0 %copy-start.36 = (f32[768]{0:T(1024)S(1)}, f32[768]{0:T(1024)}, u32[]{:S(2)}) copy-start(f32[768]{0:T(1024)} %copy-done.34) | copy-start | bytes 9220
  122.4 2.0 %copy-start.47 = (f32[1024]{0:T(1024)S(1)}, f32[1024]{0:T(1024)}, u32[]{:S(2)}) copy-start(f32[1024]{0:T(1024)} %get-tuple-element.86) | copy-start | bytes 12292
  122.4 2.0 %copy-start.49 = (f32[1024]{0:T(1024)S(1)}, f32[1024]{0:T(1024)}, u32[]{:S(2)}) copy-start(f32[1024]{0:T(1024)} %get-tuple-element.88) | copy-start | bytes 12292
  122.4 2.0 %copy-start.52 = (f32[768]{0:T(1024)S(1)}, f32[768]{0:T(1024)}, u32[]{:S(2)}) copy-start(f32[768]{0:T(1024)} %copy-done.50) | copy-start | bytes 9220
  122.4 2.2 %copy-start.65 = (bf16[1024,384]{1,0:T(8,128)(2,1)S(1)}, bf16[1024,384]{1,0:T(8,128)(2,1)}, u32[]{:S(2)}) copy-start(bf16[1024,384]{1,0:T(8,128)(2,1)} %get-tuple-element.41) | copy-start | bytes 2359300
  124.6 3.1 %copy-start.39 = (f32[32,24]{1,0:T(8,128)S(1)}, f32[32,24]{1,0:T(8,128)}, u32[]{:S(2)}) copy-start(f32[32,24]{1,0:T(8,128)} %broadcast_select_fusion) | copy-start | bytes 9220
  124.6 3.1 %copy-start.41 = (f32[32,96]{1,0:T(8,128)S(1)}, f32[32,96]{1,0:T(8,128)}, u32[]{:S(2)}) copy-start(f32[32,96]{1,0:T(8,128)} %copy-done.40) | copy-start | bytes 36868
  173.7 0.8 copy-start
  174.6 2.0 %copy-start.1 = (bf16[4,96,768]{2,1,0:T(8,128)(2,1)S(1)}, bf16[4,96,768]{2,1,0:T(8,128)(2,1)}, u32[]{:S(2)}) copy-start(bf16[4,96,768]{2,1,0:T(8,128)(2,1)} %copy-done) | copy-start | bytes 1769476
  176.6 5.6 %copy-start.63 = (f32[24]{0:T(128)}, f32[24]{0:T(128)S(1)}, u32[]{:S(2)}) copy-start(f32[24]{0:T(128)S(1)} %get-tuple-element.122) | copy-start | bytes 292
  176.6 3.3 %copy-start.13 = (bf16[1,128,768]{2,1,0:T(8,128)(2,1)S(1)}, bf16[1,128,768]{2,1,0:T(8,128)(2,1)}, u32[]{:S(2)}) copy-start(bf16[1,128,768]{2,1,0:T(8,128)(2,1)} %param.15) | copy-start | bytes 589828
  176.6 3.3 %copy-start.61 = (f32[128]{0:T(128)S(1)}, f32[128]{0:T(128)}, u32[]{:S(2)}) copy-start(f32[128]{0:T(128)} %copy-done.60) | copy-start | bytes 1540
  176.6 3.3 %copy-start.62 = (f32[128]{0:T(128)S(1)}, f32[128]{0:T(128)}, u32[]{:S(2)}) copy-start(f32[128]{0:T(128)} %add_rsqrt_fusion.1) | copy-start | bytes 1540
  176.7 3.5 %copy-start.26 = (bf16[1,128,768]{2,1,0:T(8,128)(2,1)S(1)}, bf16[1,128,768]{2,1,0:T(8,128)(2,1)}, u32[]{:S(2)}) copy-start(bf16[1,128,768]{2,1,0:T(8,128)(2,1)} %param.29) | copy-start | bytes 589828
  176.7 3.5 %copy-start.44 = (f32[768]{0:T(1024)S(1)}, f32[768]{0:T(1024)}, u32[]{:S(2)}) copy-start(f32[768]{0:T(1024)} %add.246) | copy-start | bytes 9220
  176.7 3.5 %copy-start.45 = (f32[768]{0:T(1024)S(1)}, f32[768]{0:T(1024)}, u32[]{:S(2)}) copy-start(f32[768]{0:T(1024)} %add.249) | copy-start | bytes 9220
  (4 other events, 2.5 us)

commit v2 on v1

--- a/solution.py
+++ b/solution.py
@@ -23,13 +23,7 @@
     pl.semaphore_wait(barrier, len(peers))
 
 
-def gather_kernel(N, F, G, xg, wa, wb, vec, xg_all, wa_all, wb_all, vec_all, send, recv, local):
-    s, f = lax.axis_index("seq"), lax.axis_index("fsdp")
-    grp, g = s // G, s % G
-    seq_peers = [(lax.rem(s + k, N), f) for k in range(1, N)]
-    z_peers = [(s, lax.rem(f + k, F)) for k in range(1, F)]
-    mates = [(grp * G + lax.rem(g + k, G), f) for k in range(1, G)]
-    greet(seq_peers + z_peers)
+def pusher(send, recv):
     count = [0]
 
     def push(src, dst, peer):
@@ -42,18 +36,29 @@
         copy.start()
         return copy
 
+    return push
+
+
+def gather_kernel(N, F, G, xg, wa, vec, xg_all, wa_all, vec_all, send, recv, local):
+    s, f = lax.axis_index("seq"), lax.axis_index("fsdp")
+    grp, g = s // G, lax.rem(s, G)
+    partner = (s + 1 - 2 * lax.rem(s, 2), f)
+    seq_peers = [(lax.rem(s + k, N), f) for k in range(1, N)]
+    z_peers = [(s, lax.rem(f + k, F)) for k in range(1, F)]
+    mates = [(grp * G + lax.rem(g + k, G), f) for k in range(1, G)]
+    greet(seq_peers + z_peers)
+    push = pusher(send, recv)
     own = [
         pltpu.make_async_copy(xg, xg_all.at[s], local.at[0]),
         pltpu.make_async_copy(wa, wa_all.at[g, f], local.at[1]),
-        pltpu.make_async_copy(wb, wb_all.at[f], local.at[2]),
-        pltpu.make_async_copy(vec, vec_all.at[s, f], local.at[3]),
+        pltpu.make_async_copy(vec, vec_all.at[s, f], local.at[2]),
     ]
     for copy in own:
         copy.start()
     vecs = [push(vec, vec_all.at[s, f], peer) for peer in z_peers]
+    far = [push(xg, xg_all.at[s], (lax.rem(s + k, N), f)) for k in range(2, N, 2)]
     firsts = [push(wa, wa_all.at[g, f], peer) for peer in z_peers]
-    rest = [push(xg, xg_all.at[s], peer) for peer in seq_peers]
-    rest += [push(wb, wb_all.at[f], peer) for peer in z_peers]
+    rest = [push(xg, xg_all.at[s], partner)]
     for copy in own:
         copy.wait()
     for copy in vecs:
@@ -62,40 +67,56 @@
     for copy in firsts:
         copy.wait()
     rest += [push(wa_all.at[g], wa_all.at[g], peer) for peer in mates]
+    for k, copy in zip(range(2, N, 2), far):
+        copy.wait()
+        origin = lax.rem(s + N - k, N)
+        rest.append(push(xg_all.at[origin], xg_all.at[origin], partner))
     for copy in rest:
         copy.wait()
 
 
 def scatter_kernel(
-    N, F, G, outp, tp, ga, gb, vecp, outr, tr, gar, gbr, vecr, ga_in, ga_sum, vec_in, vec_sum, send, recv
+    N, F, G, outp, tp, ga, vecp, outr, tr, gar, vecr,
+    pair_in, pair_sum, ga_in, ga_sum, vec_in, vec_sum, send, recv
 ):
     s, f = lax.axis_index("seq"), lax.axis_index("fsdp")
-    grp, g = s // G, s % G
+    grp, g = s // G, lax.rem(s, G)
+    chip, core = s // 2, lax.rem(s, 2)
+    C = N // 2
+    partner = (s + 1 - 2 * core, f)
     seq_index = [lax.rem(s + k, N) for k in range(1, N)]
     z_index = [lax.rem(f + k, F) for k in range(1, F)]
     mate_index = [lax.rem(g + k, G) for k in range(1, G)]
     greet([(p, f) for p in seq_index] + [(s, p) for p in z_index])
-    count = [0]
-
-    def push(src, dst, peer):
-        i = count[0]
-        count[0] += 1
-        copy = pltpu.make_async_remote_copy(
-            src_ref=src, dst_ref=dst, send_sem=send.at[i], recv_sem=recv.at[i],
-            device_id=peer, device_id_type=MESH,
-        )
-        copy.start()
-        return copy
-
+    push = pusher(send, recv)
+    mates = [push(ga.at[p], ga_in.at[k], (grp * G + p, f)) for k, p in enumerate(mate_index)]
+    chips = [lax.rem(chip + k, C) for k in range(1, C)] + [chip]
+    halves = []
+    for j in chips:
+        halves.append(
+            [push(a.at[2 * j + 1 - core], pair_in.at[i, j], partner) for i, a in enumerate((outp, tp))]
+        )
     vecs = [push(vecp.at[p], vec_in.at[k], (p, f)) for k, p in enumerate(seq_index)]
-    mates = [push(ga.at[p], ga_in.at[k], (grp * G + p, f)) for k, p in enumerate(mate_index)]
-    rest = [push(gb.at[p], gbr.at[f], (s, p)) for p in z_index]
-    for p in seq_index:
-        rest.append(push(outp.at[p], outr.at[s], (p, f)))
-        rest.append(push(tp.at[p], tr.at[s], (p, f)))
-    outr[s] = outp[s]
-    tr[s] = tp[s]
-    gbr[f] = gb[f]
+    rest = []
+    for copy in mates:
+        copy.wait()
+    for i in range(F):
+        part = ga[g, i].astype(F32)
+        for k in range(G - 1):
+            part = part + ga_in[k, i].astype(F32)
+        ga_sum[i] = part.astype(BF)
+    rest += [push(ga_sum.at[p], gar.at[f], (s, p)) for p in z_index]
+    waits = []
+    for n, j in enumerate(chips):
+        for i, (a, out) in enumerate(((outp, outr), (tp, tr))):
+            halves[n][i].wait()
+            both = (a[2 * j + core].astype(F32) + pair_in[i, j].astype(F32)).astype(BF)
+            if n == C - 1:
+                out[chip] = both
+            else:
+                pair_sum[i, j] = both
+                waits.append(push(pair_sum.at[i, j], out.at[chip], (2 * j + core, f)))
+    gar[f] = ga_sum[f]
     for copy in vecs:
         copy.wait()
     total = vecp[s]
@@ -104,56 +125,52 @@
     vec_sum[...] = total
     rest += [push(vec_sum.at[p], vecr.at[f], (s, p)) for p in z_index]
     vecr[f] = vec_sum[f]
-    for copy in mates:
-        copy.wait()
-    for i in range(F):
-        part = ga[g, i].astype(F32)
-        for k in range(G - 1):
-            part = part + ga_in[k, i].astype(F32)
-        ga_sum[i] = part.astype(BF)
-    rest += [push(ga_sum.at[p], gar.at[f], (s, p)) for p in z_index]
-    gar[f] = ga_sum[f]
-    for copy in rest:
-        copy.wait()
-
-
-def gather_phase(N, F, G, xg, wa, wb, vec):
-    copies = 3 * (F - 1) + 2 * (N - 1) + G - 1
+    for copy in rest + waits:
+        copy.wait()
+
+
+COST = pl.CostEstimate(flops=0, bytes_accessed=80 * 10**6, transcendentals=0)
+
+
+def gather_phase(N, F, G, xg, wa, vec):
+    copies = 2 * (F - 1) + 2 * (N - 1) + G - 1
     hbm = pl.BlockSpec(memory_space=pl.ANY)
     return pl.pallas_call(
         lambda *refs: gather_kernel(N, F, G, *refs),
         out_shape=(
             jax.ShapeDtypeStruct((N,) + xg.shape, xg.dtype),
             jax.ShapeDtypeStruct((G, F) + wa.shape, wa.dtype),
-            jax.ShapeDtypeStruct((F,) + wb.shape, wb.dtype),
             jax.ShapeDtypeStruct((N, F) + vec.shape, vec.dtype),
         ),
-        in_specs=[hbm] * 4,
-        out_specs=(hbm,) * 4,
+        in_specs=[hbm] * 3,
+        out_specs=(hbm,) * 3,
         scratch_shapes=[
             pltpu.SemaphoreType.DMA((copies,)),
             pltpu.SemaphoreType.DMA((copies,)),
-            pltpu.SemaphoreType.DMA((4,)),
+            pltpu.SemaphoreType.DMA((3,)),
         ],
         compiler_params=pltpu.CompilerParams(collective_id=0, has_side_effects=True),
-    )(xg, wa, wb, vec)
-
-
-def scatter_phase(N, F, G, outp, tp, ga, gb, vecp):
-    copies = 3 * (F - 1) + 3 * (N - 1) + G - 1
+        cost_estimate=COST,
+    )(xg, wa, vec)
+
+
+def scatter_phase(N, F, G, outp, tp, ga, vecp):
+    copies = 2 * (F - 1) + 3 * N + G
     vmem = pl.BlockSpec(memory_space=pltpu.VMEM)
+    half = (N // 2,) + outp.shape[1:]
     return pl.pallas_call(
         lambda *refs: scatter_kernel(N, F, G, *refs),
         out_shape=(
-            jax.ShapeDtypeStruct(outp.shape, BF),
-            jax.ShapeDtypeStruct(tp.shape, BF),
+            jax.ShapeDtypeStruct(half, BF),
+            jax.ShapeDtypeStruct(half, BF),
             jax.ShapeDtypeStruct(ga.shape[1:], BF),
-            jax.ShapeDtypeStruct(gb.shape, BF),
             jax.ShapeDtypeStruct(vecp.shape[1:], F32),
         ),
-        in_specs=[vmem] * 5,
-        out_specs=(vmem,) * 5,
+        in_specs=[vmem] * 4,
+        out_specs=(vmem,) * 4,
         scratch_shapes=[
+            pltpu.VMEM((2,) + half, BF),
+            pltpu.VMEM((2,) + half, BF),
             pltpu.VMEM((max(G - 1, 1),) + ga.shape[1:], BF),
             pltpu.VMEM(ga.shape[1:], BF),
             pltpu.VMEM((N - 1,) + vecp.shape[1:], F32),
@@ -164,7 +181,14 @@
         compiler_params=pltpu.CompilerParams(
             collective_id=1, has_side_effects=True, vmem_limit_bytes=48 * 2**20
         ),
-    )(outp, tp, ga, gb, vecp)
+        cost_estimate=COST,
+    )(outp, tp, ga, vecp)
+
+
+def lane_rows(arrays):
+    spread = [jnp.pad(a, [(0, 0)] * (a.ndim - 1) + [(0, 128 - a.shape[-1])]) for a in arrays]
+    spread += [jnp.zeros_like(spread[0])] * (8 - len(spread))
+    return jnp.stack(spread, axis=-2)
 
 
 def row_places(pair_held, count, block_rows):
@@ -217,38 +241,38 @@
         W = HG * HD
         Q = L // G
         cj, cd, ce = joint_weight.shape[1], dense_weight.shape[0], expand_weight.shape[1]
-        s = lax.axis_index("seq")
+        s, f = lax.axis_index("seq"), lax.axis_index("fsdp")
         grp, gi = s // G, s % G
         scale = HD ** (-0.5)
 
         xg = jnp.concatenate([tokens, cotangent], axis=0)
         wa = pad_rows(jnp.concatenate([joint_weight.T, dense_weight], axis=0), 0)
         wb = pad_rows(jnp.concatenate([expand_weight.T, reduce_weight], axis=0), 0)
-        vec = jnp.concatenate(
-            [first_gain, first_shift, second_gain, second_shift, joint_bias, dense_bias,
-             expand_bias, reduce_bias]
-        ).astype(F32)
-        vec = jnp.pad(vec, (0, 1024 - vec.shape[0])).reshape(8, 128)
-        xg_all, wa_all, wb_all, vec_all = gather_phase(N, F, G, xg, wa, wb, vec)
-
-        va = vec_all.reshape(N * F, 1024)
-        gain1, shift1, gain2, shift2 = [
-            va[:, i * cd:(i + 1) * cd].reshape(D) for i in range(4)
+        vec = lane_rows(
+            [array.astype(F32) for array in (
+                first_gain, first_shift, second_gain, second_shift, joint_bias, dense_bias,
+                expand_bias, reduce_bias)]
+        )
+        wb_list = [wb] + [
+            lax.ppermute(wb, "fsdp", [(i, (i + k) % F) for i in range(F)]) for k in range(1, F)
         ]
-        at = 4 * cd
-        bias_j = lax.dynamic_slice_in_dim(va[:, at:at + cj], grp * G * F, G * F, 0).reshape(HG, 3, HD)
-        at += cj
-        bias_d = va[:, at:at + cd].reshape(D)
-        at += cd
-        bias_e = lax.dynamic_slice_in_dim(va[:, at:at + ce], s * F, F, 0).reshape(F * ce)
-        at += ce
-        bias_r = va[:, at:at + cd].reshape(D)
+        xg_all, wa_all, vec_all = gather_phase(N, F, G, xg, wa, vec)
+
+        va = vec_all.reshape(N * F, 8, 128)
+        gain1, shift1, gain2, shift2, _, bias_d, _, bias_r = [
+            va[:, i, :cd].reshape(D) for i in range(8)
+        ]
+        bias_j = lax.dynamic_slice_in_dim(va[:, 4, :cj], grp * G * F, G * F, 0).reshape(HG, 3, HD)
+        places_f = jnp.arange(F)
+        turned = (places_f[None, :] == (f - places_f[:, None] + F) % F)[:, :, None]
+        bias_e = lax.dynamic_slice_in_dim(va[:, 6, :ce], s * F, F, 0)
+        bias_e = jnp.sum(jnp.where(turned, bias_e[None], 0.0), axis=1).reshape(F * ce)
 
         joint = wa_all[:, :, :cj].reshape(HG, 3, HD, D)
         wq, wk, wv = [joint[:, i].reshape(W, D) for i in range(3)]
         dense = wa_all[:, :, cj:cj + cd].reshape(W, D)
-        expand = wb_all[:, :ce].reshape(F * ce, D)
-        reduce_w = wb_all[:, ce:2 * ce].reshape(F * ce, D)
+        expand = jnp.concatenate([w[:ce] for w in wb_list], axis=0)
+        reduce_w = jnp.concatenate([w[ce:2 * ce] for w in wb_list], axis=0)
 
         x = xg_all[:, 0].reshape(L, D).astype(F32)
         grad = xg_all[:, 1].reshape(L, D)
@@ -286,6 +310,20 @@
         probs = probs_full.astype(BF)
         context = jnp.einsum("hqk,khd->qhd", probs, v, preferred_element_type=F32)
         ctx_low = context.reshape(Q, W).astype(BF)
+        nf2_late, ctx_low = lax.optimization_barrier((nf2, ctx_low))
+        hidden = nt(nf2_late, expand) + bias_e
+        active, gelu_pull = jax.vjp(lambda t: jax.nn.gelu(t, approximate=False), hidden)
+        active = active.astype(BF)
+        g_hidden = gelu_pull(nt(grad, reduce_w))[0].astype(BF)
+        gb = pad_rows(
+            jnp.concatenate(
+                [tn(g_hidden, nf2).astype(BF).reshape(F, ce, D),
+                 tn(active, grad).astype(BF).reshape(F, ce, D)], axis=1), 1
+        )
+        gctx, gb = lax.optimization_barrier((gctx, gb))
+        b_parts = [gb[0]] + [
+            lax.ppermute(gb[k], "fsdp", [(i, (i - k) % F) for i in range(F)]) for k in range(1, F)
+        ]
         g_probs = jnp.einsum("qhd,khd->hqk", gctx, v, preferred_element_type=F32)
         delta = jnp.sum(probs_full * g_probs, axis=-1, keepdims=True)
         g_scores = (probs_full * (g_probs - delta)).astype(BF)
@@ -296,11 +334,7 @@
         gk = turn(gk, cosine, -sine).astype(BF).reshape(L, W)
         gv = gv.astype(BF).reshape(L, W)
 
-        hidden = nt(nf2, expand) + bias_e
-        active, gelu_pull = jax.vjp(lambda t: jax.nn.gelu(t, approximate=False), hidden)
-        active = active.astype(BF)
         out_part = nn(active, reduce_w) + own_rows(nn(ctx_low, dense))
-        g_hidden = gelu_pull(nt(grad, reduce_w))[0].astype(BF)
         g2 = nn(g_hidden, expand)
         g1 = nn(gk, wk) + nn(gv, wv) + own_rows(nn(gq, wq))
         t_part = g1 * gain1 + g2 * gain2
@@ -311,11 +345,6 @@
         ).reshape(G, F, cj, D)
         d_dense = tn(ctx_low, grad_q).astype(BF).reshape(G, F, cd, D)
         ga = pad_rows(jnp.concatenate([d_joint, d_dense], axis=2), 2)
-        gb = pad_rows(
-            jnp.concatenate(
-                [tn(g_hidden, nf2).astype(BF).reshape(F, ce, D),
-                 tn(active, grad).astype(BF).reshape(F, ce, D)], axis=1), 1
-        )
 
         def col(array):
             return jnp.sum(array.astype(F32), axis=0)
@@ -328,15 +357,15 @@
         b_joint = jnp.stack([col(a).reshape(HG, HD) for a in (gq, gk, gv)], axis=1).reshape(G * F, cj)
         b_joint = lax.dynamic_update_slice_in_dim(jnp.zeros((N * F, cj), F32), b_joint, grp * G * F, 0)
         b_expand = lax.dynamic_update_slice_in_dim(
-            jnp.zeros((N * F, ce), F32), col(g_hidden).reshape(F, ce), s * F, 0
+            jnp.zeros((N * F, ce), F32),
+            jnp.sum(jnp.where(turned, col(g_hidden).reshape(1, F, ce), 0.0), axis=1), s * F, 0
         )
         b_out = jnp.where((owner_s == s)[:, None], col(grad).reshape(N * F, cd), 0.0)
-        vecp = jnp.concatenate(gains + [b_joint, b_out, b_expand], axis=1)
-        vecp = jnp.pad(vecp, ((0, 0), (0, 1024 - vecp.shape[1]))).reshape(N, F, 8, 128)
-
-        outr, tr, gar, gbr, vecr = scatter_phase(
+        vecp = lane_rows(gains + [b_joint, b_out, b_expand]).reshape(N, F, 8, 128)
+
+        outr, tr, gar, vecr = scatter_phase(
             N, F, G, out_part.astype(BF).reshape(N, R, D), t_part.astype(BF).reshape(N, R, D),
-            ga, gb, vecp
+            ga, vecp
         )
         x_own = tokens[0].astype(F32)
         layer_output = (x_own + jnp.sum(outr.astype(F32), axis=0) + bias_d + bias_r).astype(BF)
@@ -350,16 +379,13 @@
         ) * inv_own
         input_grad = (cotangent[0].astype(F32) + g_in).astype(BF)
         a = jnp.sum(gar.astype(F32), axis=0)
-        b = jnp.sum(gbr.astype(F32), axis=0)
-        vs = jnp.sum(vecr, axis=0).reshape(1024)
-        at = 4 * cd
-        o_joint, at = vs[at:at + cj], at + cj
-        o_out, at = vs[at:at + cd], at + cd
-        o_expand = vs[at:at + ce]
+        b = sum(part.astype(F32) for part in b_parts)
+        vs = jnp.sum(vecr, axis=0)
+        o_joint, o_out, o_expand = vs[4, :cj], vs[5, :cd], vs[6, :ce]
         return (
             layer_output[None], input_grad[None], a[:cj].T, o_joint, a[cj:cj + cd], o_out,
             b[:ce].T, o_expand, b[ce:2 * ce], o_out,
-            vs[:cd], vs[cd:2 * cd], vs[2 * cd:3 * cd], vs[3 * cd:4 * cd],
+            vs[0, :cd], vs[1, :cd], vs[2, :cd], vs[3, :cd],
         )
 
     return body

time: 183 us -> 216 us (1.18)
  Pallas kernels: 89.1 us -> 61.4 us
  local copies, waits for them, and re-layouts: 26.6 us -> 48.9 us
  waiting for transfers between devices: 0 us -> 22.1 us
  starting transfers between devices: 0 us -> 8.71 us
  matrix products: 38.9 us -> 42.7 us
  other arithmetic: 26.3 us -> 28.8 us
    ppermute x0 -> x6, waiting for transfers between devices: none -> 22.1 us  [the longest x3 22.1 us: body(): lax.ppermute(gb[k], 'fsdp', [(i, (i - k) % F) for i in range(F)])]
    pallas_call x1, Pallas kernels: 45.8 us -> 29.8 us  [scatter_phase(): pl.pallas_call(lambda *refs: scatter_kernel(N, F, G, *refs), out_shape=(j...]
    pallas_call x1, Pallas kernels: 43.3 us -> 31.6 us  [gather_phase(): pl.pallas_call(lambda *refs: gather_kernel(N, F, G, *refs), out_shape=(ja...]
    ppermute x0 -> x6, starting transfers between devices: none -> 8.71 us  [the longest x3 6.06 us: body(): lax.ppermute(wb, 'fsdp', [(i, (i + k) % F) for i in range(F)])]
    slice x7 -> x6, local copies, waits for them, and re-layouts: 2.06 us -> 7.84 us  [the longest x3 3.19 us: body(): reduce_w = jnp.concatenate([w[ce:2 * ce] for w in wb_list], axis=0)]
    concatenate x2 -> x0, local copies, waits for them, and re-layouts: 5.53 us -> none  [the longest x1 5.44 us: body(): jnp.concatenate([first_gain, first_shift, second_gain, second_shift, join...]
    pad x0 -> x7, local copies, waits for them, and re-layouts: none -> 3.67 us  [lane_rows(): jnp.pad(a, [(0, 0)] * (a.ndim - 1) + [(0, 128 - a.shape[-1])])]
    another operation x0 -> x7, local copies, waits for them, and re-layouts: none -> 3.59 us  [lane_rows(): return jnp.stack(spread, axis=-2)]
  transfers between devices with their start and end apart: 0 -> 6, of which waited for: 0 -> 3; matrix products, arithmetic and copies ran while one was open for 0% -> 32% of each run, Pallas kernels for 0% -> 15%
where the time goes in v2:
time: 216 us; the launch traced here: 215 us
  Pallas kernels  61.4 us (28%)
  local copies, waits for them, and re-layouts  48.9 us (23%)
  matrix products  42.7 us (20%)
  other arithmetic  28.8 us (13%)
  waiting for transfers between devices  22.1 us (10%)
  starting transfers between devices  8.71 us (4%)
    pallas_call x1, Pallas kernels, gather_phase(): pl.pallas_call(lambda *refs: gather_kernel(N, F, G, *refs), out_shape=(ja...  31.6 us
    pallas_call x1, Pallas kernels, scatter_phase(): pl.pallas_call(lambda *refs: scatter_kernel(N, F, G, *refs), out_shape=(j...  29.8 us
    ppermute x3, waiting for transfers between devices, body(): lax.ppermute(gb[k], 'fsdp', [(i, (i - k) % F) for i in range(F)])  22.1 us
    dot_general x6, matrix products, nt(): lax.dot_general(left, right, (((1,), (1,)), ((), ())), preferred_element_...  13.5 us
    unnamed x218, local copies, waits for them, and re-layouts  10.9 us
    dot_general x6, matrix products, nn(): return jnp.dot(left, right, preferred_element_type=F32)  8.09 us
    ppermute x3, starting transfers between devices, body(): lax.ppermute(wb, 'fsdp', [(i, (i + k) % F) for i in range(F)])  6.06 us
    dot_general x6, matrix products, tn(): lax.dot_general(left, right, (((0,), (0,)), ((), ())), preferred_element_...  5.53 us
  transfers between devices with their start and end apart: 6, of which 3 were waited for; matrix products, arithmetic and copies ran while one was open for 32% of the time, Pallas kernels for 15%

profile of v2, /device:TPU:0, one launch (start us, length us, event | category | flops | bytes accessed | tf_op | source)
XLA Modules:
  0.0 214.6 jit_solution(5624272066021523749)
XLA Ops:
  0.7 1.8 pad_maximum_fusion.8
  2.4 5.0 %collective-permute-start.2 = (bf16[192,768]{1,0:T(8,128)(2,1)}, bf16[192,768]{1,0:T(8,128)(2,1)}, u32[]{:S(2)}, u32[]{:S(2)}) collective-permute-start(bf16[192,768]{1,0:T(8,128)(2,1)} %pad_maximum_fusion.8), channel_id=1, source_target_pairs={{0,3},{1,0},{2,1},{3,2},{4,7},{5,4},{6,5},{7,6},{8,11},{9,8},{10,9... | collective-permute-start | bytes 884744 | tf_op jit(solution)/shard_map/ppermute | solution.py:257
  7.5 1.0 collective-permute-start
  9.0 1.6 convert_reduce_fusion.9
  13.9 1.8 pad_maximum_fusion.5.refs_0_
  16.4 31.6 %shard_map.254 = (bf16[8,2,128,768]{3,2,1,0:T(8,128)(2,1)}, bf16[2,4,96,768]{3,2,1,0:T(8,128)(2,1)}, f32[8,4,8,128]{3,2,1,0:T(8,128)}) custom-call(bf16[2,128,768]{2,1,0:T(8,128)(2,1)} %pad_maximum_fusion.5.refs_0_, bf16[96,768]{1,0:T(8,128)(2,1)} %pad_maximum_fusion.10.refs_1_, f32[8,128]{1,0:T(8,128)} %stack.85.refs_2_), custom_call_target="tpu_custom_call" | custom-call | bytes 80000000 | tf_op jit(solution)/shard_map/pallas_call | solution.py:138
  48.0 0.9 slice.212
  48.9 1.5 slice.227
  50.4 2.2 %fusion.84 = (f32[32,1,24]{2,1,0:T(1,128)}, f32[32,1,24]{2,1,0:T(1,128)S(1)}, f32[32,1,24]{2,1,0:T(1,128)S(1)}, f32[32,1,24]{2,1,0:T(1,128)}, f32[32,1,24]{2,1,0:T(1,128)}, /*index=5*/f32[32,1,24]{2,1,0:T(1,128)}) fusion(f32[32,8,128]{2,1,0:T(8,128)} %bitcast.265), kind=kLoop, calls=%fused_computation.209 | loop fusion | bytes 36864 | tf_op jit(solution)/shard_map/slice | solution.py:263
  52.6 1.0 slice.182
  53.6 2.3 %slice.161 = bf16[2,4,72,768]{3,2,1,0:T(8,128)(2,1)} slice(bf16[2,4,96,768]{3,2,1,0:T(8,128)(2,1)} %get-tuple-element.27), slice={[0:2], [0:4], [0:72], [0:768]} | slice | bytes 1769472 | tf_op jit(solution)/shard_map/slice | solution.py:271
  57.5 1.7 convert_reduce_fusion.1
  59.7 1.4 convert_reduce_fusion
  62.6 2.1 fusion.79
  64.7 0.8 fusion.59
  66.8 1.8 convolution_add_fusion.1
  69.5 1.3 slice.183
  70.8 1.2 broadcast_compare_fusion
  73.2 1.4 mul.325
  74.5 1.4 add.256
  76.0 2.9 %fusion.22 = bf16[1024,3,64]{0,2,1:T(8,128)(2,1)} fusion(bf16[1024,768,1]{1,0,2:T(8,128)(2,1)} %bitcast.228, f32[3,64]{1,0:T(4,128)} %bitcast.284, bf16[3,3,64,768]{3,2,1,0:T(8,128)(2,1)} %bitcast.235), kind=kOutput, calls=%fused_computation.60 | convolution fusion | flops 302383104 | bytes 2263040 | tf_op jit(solution)/shard_map/dot_general | solution.py:210
  78.9 1.8 fusion.5
  80.7 1.8 copy-done.10
  82.5 1.4 convolution_add_fusion.3
  84.0 4.9 %fusion.86 = (f32[3,512]{1,0:T(4,128)S(1)}, f32[3,512,1024]{2,1,0:T(8,128)}) fusion(pred[512,1024]{1,0:T(8,128)(4,1)S(1)} %copy-done.41, bf16[512,3,48]{0,2,1:T(8,128)(2,1)S(1)} %slice.300, bf16[512,3,8]{0,2,1:T(8,128)(2,1)S(1)} %get-tuple-element.70, bf16[512,3,8]{0,2,1:T(8,128)(2,1)S(1)} %get-tuple-element.69, bf16[1024,3,48]{0,2,1:T(8,128)(2,1)S(1)} %copy-done.26, ...), kind=kOutput, calls=%fused_computation.211 | convolution fusion | flops 209388544 | bytes 7411712 | tf_op jit(solution)/shard_map/sub | solution.py:308
  89.0 4.1 %fusion.27 = bf16[3,64,512]{2,1,0:T(8,128)(2,1)S(1)} fusion(bf16[1024,3,64]{0,2,1:T(8,128)(2,1)S(1)} %copy-done.103, f32[3,512,1024]{2,1,0:T(8,128)} %get-tuple-element.101, f32[3,512]{1,0:T(4,128)S(1)} %get-tuple-element.100), kind=kOutput, calls=%fused_computation.72 | convolution fusion | flops 204570624 | bytes 6887424 | tf_op jit(solution)/shard_map/hqk,khd->qhd/dot_general | solution.py:311
  93.1 1.1 convolution_convert_fusion.6
  94.2 1.1 convolution_convert_fusion.4
  95.3 2.5 %fusion.87 = f32[512,768]{1,0:T(8,128)} fusion(bf16[512,192]{0,1:T(8,128)(2,1)S(1)} %bitcast.257, bf16[192,768]{1,0:T(8,128)(2,1)} %bitcast.241), kind=kOutput, calls=%fused_computation.212 | convolution fusion | flops 150994944 | bytes 2064384 | tf_op jit(solution)/shard_map/dot_general | solution.py:214
  102.5 1.3 add_rsqrt_fusion.1
  106.5 1.0 fusion.83
  107.5 1.1 fusion.82
  108.7 1.1 fusion.81
  109.8 4.3 %multiply_convert_fusion.1 = (bf16[1024,384]{1,0:T(8,128)(2,1)S(1)}, f32[1024,384]{1,0:T(8,128)S(1)}, f32[1024,384]{1,0:T(8,128)S(1)}) fusion(f32[384]{0:T(512)S(1)} %add.285, bf16[1024,768]{1,0:T(8,128)(2,1)S(1)} %copy-done.13, bf16[96,768]{1,0:T(8,128)(2,1)S(1)} %get-tuple-element.76, bf16[96,768]{1,0:T(8,128)(2,1)S(1)} %get-tuple-element.74, ...), kind=kOutput, calls=%fused_computation.35 | convolution fusion | flops 632291328 | bytes 6096384 | tf_op jit(solution)/shard_map/dot_general | solution.py:210
  114.2 0.9 copy-done.16
  115.1 0.8 convolution_convert_fusion
  115.9 2.0 convert_reduce_fusion.5
  117.9 0.8 convolution_convert_fusion.1
  118.8 1.1 pad_maximum_fusion
  119.9 2.1 %convert_reduce_fusion.7 = (f32[3,64]{1,0:T(4,128)}, bf16[3,64,1024]{2,1,0:T(8,128)(2,1)}) fusion(bf16[512,3,64]{0,2,1:T(8,128)(2,1)S(1)} %bitcast.258, f32[3,512,1024]{2,1,0:T(8,128)S(1)} %bitcast.232, f32[3,512]{1,0:T(4,128)S(1)} %copy-done.91), kind=kOutput, calls=%fused_computation.77 | convolution fusion | flops 205061952 | bytes 6888192 | tf_op jit(solution)/shard_map/hqk,qhd->khd/dot_general | solution.py:332
  122.1 1.8 multiply_reduce_fusion
  123.9 1.1 multiply_convert_fusion
  125.0 1.1 fusion.26
  126.1 1.6 fusion.21
  127.7 1.3 broadcast_in_dim.140
  129.1 0.8 select_reduce_fusion
  132.2 1.9 convolution_convert_fusion.5
  138.1 1.0 fusion.4
  140.0 1.1 copy-done.6
  141.4 2.8 %multiply_reduce_fusion.1 = (f32[768]{0:T(1024)S(1)}, f32[768]{0:T(1024)S(1)}, f32[768]{0:T(1024)S(1)}, f32[768]{0:T(1024)S(1)}, bf16[1024,768]{1,0:T(8,128)(2,1)}) fusion(f32[1024]{0:T(1024)S(1)} %copy-done.83, f32[1024]{0:T(1024)S(1)} %copy-done.81, bf16[8,2,128,768]{3,2,1,0:T(8,128)(2,1)S(1)} %copy-done.6, f32[1024,768]{1,0:T(8,128)S(1)} %fusion.2, ...), kind=kOutput, calls=%fused_computation.14 | convolution fusion | flops 616559616 | bytes 7694336 | tf_op jit(solution)/shard_map/dot_general | solution.py:214
  147.1 1.1 pad_maximum_fusion.1.refs_2_
  148.3 0.8 stack.98.refs_3_
  149.1 0.9 copy-done.4
  150.0 29.8 %shard_map.255 = (bf16[4,128,768]{2,1,0:T(8,128)(2,1)S(1)}, bf16[4,128,768]{2,1,0:T(8,128)(2,1)S(1)}, bf16[4,96,768]{2,1,0:T(8,128)(2,1)S(1)}, f32[4,8,128]{2,1,0:T(8,128)S(1)}) custom-call(bf16[8,128,768]{2,1,0:T(8,128)(2,1)S(1)} %bitcast.222, bf16[8,128,768]{2,1,0:T(8,128)(2,1)} %bitcast.248, bf16[2,4,96,768]{3,2,1,0:T(8,128)(2,1)S(1)} %pad_maximum_fusion.1.refs_2_, ...), custom_call_target="tpu_custom_call" | custom-call | bytes 80000000 | tf_op jit(solution)/shard_map/pallas_call | solution.py:161
  179.9 0.9 copy-done
  183.2 1.2 slice_bitcast_fusion.3
  184.4 1.0 collective-permute-start.3
  185.5 1.1 collective-permute-start.5
  189.1 0.9 fusion.45
  190.0 9.5 %collective-permute-done.3 = bf16[192,768]{1,0:T(8,128)(2,1)S(1)} collective-permute-done((bf16[192,768]{1,0:T(8,128)(2,1)S(1)}, bf16[192,768]{1,0:T(8,128)(2,1)S(1)}, u32[]{:S(2)}, u32[]{:S(2)}) %collective-permute-start.3) | collective-permute-done | bytes 294944 | tf_op jit(solution)/shard_map/ppermute | solution.py:325
  199.5 1.3 collective-permute-done.5
  200.8 11.3 %collective-permute-done.4 = bf16[192,768]{1,0:T(8,128)(2,1)S(1)} collective-permute-done((bf16[192,768]{1,0:T(8,128)(2,1)S(1)}, bf16[192,768]{1,0:T(8,128)(2,1)S(1)}, u32[]{:S(2)}, u32[]{:S(2)}) %collective-permute-start.4) | collective-permute-done | bytes 294944 | tf_op jit(solution)/shard_map/ppermute | solution.py:325
  212.2 1.1 fusion.36
  213.3 0.8 fusion.80
  (308 shorter events, 34.6 us)
Async XLA Ops:
  0.6 15.1 %copy-start.79 = (bf16[24,768]{1,0:T(8,128)(2,1)S(1)}, bf16[24,768]{1,0:T(8,128)(2,1)}, u32[]{:S(2)}) copy-start(bf16[24,768]{1,0:T(8,128)(2,1)} %param.19) | copy-start | bytes 110596
  0.7 15.1 %copy-start.58 = (bf16[768,72]{0,1:T(8,128)(2,1)S(1)}, bf16[768,72]{0,1:T(8,128)(2,1)}, u32[]{:S(2)}) copy-start(bf16[768,72]{0,1:T(8,128)(2,1)} %param.17) | copy-start | bytes 331780
  2.4 104.1 %collective-permute-start.2 = (bf16[192,768]{1,0:T(8,128)(2,1)}, bf16[192,768]{1,0:T(8,128)(2,1)}, u32[]{:S(2)}, u32[]{:S(2)}) collective-permute-start(bf16[192,768]{1,0:T(8,128)(2,1)} %pad_maximum_fusion.8), channel_id=1, source_target_pairs={{0,3},{1,0},{2,1},{3,2},{4,7},{5,4},{6,5},{7,6},{8,11},{9,8},{10,9... | collective-permute-start | bytes 884744 | tf_op jit(solution)/shard_map/ppermute | solution.py:257
  7.5 100.1 %collective-permute-start.1 = (bf16[192,768]{1,0:T(8,128)(2,1)}, bf16[192,768]{1,0:T(8,128)(2,1)}, u32[]{:S(2)}, u32[]{:S(2)}) collective-permute-start(bf16[192,768]{1,0:T(8,128)(2,1)} %pad_maximum_fusion.8), channel_id=1, source_target_pairs={{0,2},{1,3},{2,0},{3,1},{4,6},{5,7},{6,4},{7,5},{8,10},{9,11},{10,... | collective-permute-start | bytes 884744 | tf_op jit(solution)/shard_map/ppermute | solution.py:257
  7.5 101.2 %collective-permute-start = (bf16[192,768]{1,0:T(8,128)(2,1)}, bf16[192,768]{1,0:T(8,128)(2,1)}, u32[]{:S(2)}, u32[]{:S(2)}) collective-permute-start(bf16[192,768]{1,0:T(8,128)(2,1)} %pad_maximum_fusion.8), channel_id=1, source_target_pairs={{0,1},{1,2},{2,3},{3,0},{4,5},{5,6},{6,7},{7,4},{8,9},{9,10},{10,1... | collective-permute-start | bytes 884744 | tf_op jit(solution)/shard_map/ppermute | solution.py:257
  16.4 40.1 %copy-start.102 = (s32[8]{0:T(128)S(1)}, s32[8]{0:T(128)}, u32[]{:S(2)}) copy-start(s32[8]{0:T(128)} %param.16) | copy-start | bytes 100
  53.6 39.4 %copy-start.19 = (bf16[2,4,24,768]{3,2,1,0:T(8,128)(2,1)}, bf16[2,4,24,768]{3,2,1,0:T(8,128)(2,1)S(1)}, u32[]{:S(2)}) copy-start(bf16[2,4,24,768]{3,2,1,0:T(8,128)(2,1)S(1)} %slice.182) | copy-start | bytes 884740
  53.6 6.1 %copy-start.5 = (bf16[8,2,128,768]{3,2,1,0:T(8,128)(2,1)S(1)}, bf16[8,2,128,768]{3,2,1,0:T(8,128)(2,1)}, u32[]{:S(2)}) copy-start(bf16[8,2,128,768]{3,2,1,0:T(8,128)(2,1)} %get-tuple-element.25) | copy-start | bytes 9437188
  56.8 4.3 %copy-start.77 = (s32[1024]{0:T(1024)}, s32[1024]{0:T(1024)S(1)}, u32[]{:S(2)}) copy-start(s32[1024]{0:T(1024)S(1)} %add.269) | copy-start | bytes 12292
  62.5 4.3 %copy-start.66 = (f32[768]{0:T(1024)}, f32[768]{0:T(1024)S(1)}, u32[]{:S(2)}) copy-start(f32[768]{0:T(1024)S(1)} %add.259) | copy-start | bytes 9220
  62.6 4.2 %copy-start.63 = (f32[768]{0:T(1024)}, f32[768]{0:T(1024)S(1)}, u32[]{:S(2)}) copy-start(f32[768]{0:T(1024)S(1)} %mul.330) | copy-start | bytes 9220
  65.5 3.2 %copy-start.42 = (f32[1024,8]{0,1:T(8,128)}, f32[1024,8]{0,1:T(8,128)S(1)}, u32[]{:S(2)}) copy-start(f32[1024,8]{0,1:T(8,128)S(1)} %get-tuple-element.90) | copy-start | bytes 98308
  68.7 15.2 %copy-start.44 = (bf16[1024,3,8]{0,2,1:T(8,128)(2,1)}, bf16[1024,3,8]{0,2,1:T(8,128)(2,1)S(1)}, u32[]{:S(2)}) copy-start(bf16[1024,3,8]{0,2,1:T(8,128)(2,1)S(1)} %get-tuple-element.63) | copy-start | bytes 147460
  68.7 15.2 %copy-start.46 = (bf16[1024,3,8]{0,2,1:T(8,128)(2,1)}, bf16[1024,3,8]{0,2,1:T(8,128)(2,1)S(1)}, u32[]{:S(2)}) copy-start(bf16[1024,3,8]{0,2,1:T(8,128)(2,1)S(1)} %get-tuple-element.64) | copy-start | bytes 147460
  69.5 2.5 %copy-start.95 = (f32[3,1,64]{2,1,0:T(1,128)S(1)}, f32[3,1,64]{2,1,0:T(1,128)}, u32[]{:S(2)}) copy-start(f32[3,1,64]{2,1,0:T(1,128)} %get-tuple-element.86) | copy-start | bytes 2308
  69.5 3.1 %copy-start.94 = (f32[3,1,64]{2,1,0:T(1,128)S(1)}, f32[3,1,64]{2,1,0:T(1,128)}, u32[]{:S(2)}) copy-start(f32[3,1,64]{2,1,0:T(1,128)} %get-tuple-element.87) | copy-start | bytes 2308
  75.9 2.9 %copy-start.80 = (f32[1024]{0:T(1024)S(1)}, f32[1024]{0:T(1024)}, u32[]{:S(2)}) copy-start(f32[1024]{0:T(1024)} %get-tuple-element.98) | copy-start | bytes 12292
  75.9 2.9 %copy-start.82 = (f32[1024]{0:T(1024)S(1)}, f32[1024]{0:T(1024)}, u32[]{:S(2)}) copy-start(f32[1024]{0:T(1024)} %get-tuple-element.97) | copy-start | bytes 12292
  75.9 2.9 %copy-start.86 = (f32[768]{0:T(1024)S(1)}, f32[768]{0:T(1024)}, u32[]{:S(2)}) copy-start(f32[768]{0:T(1024)} %mul.325) | copy-start | bytes 9220
  75.9 2.9 %copy-start.88 = (f32[768]{0:T(1024)S(1)}, f32[768]{0:T(1024)}, u32[]{:S(2)}) copy-start(f32[768]{0:T(1024)} %add.256) | copy-start | bytes 9220
  78.8 3.6 %copy-start.64 = (f32[768]{0:T(1024)S(1)}, f32[768]{0:T(1024)}, u32[]{:S(2)}) copy-start(f32[768]{0:T(1024)} %copy-done.63) | copy-start | bytes 9220
  78.9 3.6 %copy-start.67 = (f32[768]{0:T(1024)S(1)}, f32[768]{0:T(1024)}, u32[]{:S(2)}) copy-start(f32[768]{0:T(1024)} %copy-done.66) | copy-start | bytes 9220
  78.9 3.6 %copy-start.93 = (f32[3,1,64]{2,0,1:T(4,128)S(1)}, f32[3,1,64]{2,0,1:T(4,128)}, u32[]{:S(2)}) copy-start(f32[3,1,64]{2,0,1:T(4,128)} %copy.82) | copy-start | bytes 2308
  80.7 3.2 %copy-start.76 = (f32[512,8]{0,1:T(8,128)S(1)}, f32[512,8]{0,1:T(8,128)}, u32[]{:S(2)}) copy-start(f32[512,8]{0,1:T(8,128)} %get-tuple-element.49) | copy-start | bytes 49156
  80.7 3.3 %copy-start.26 = (bf16[1024,3,48]{0,2,1:T(8,128)(2,1)S(1)}, bf16[1024,3,48]{0,2,1:T(8,128)(2,1)}, u32[]{:S(2)}) copy-start(bf16[1024,3,48]{0,2,1:T(8,128)(2,1)} %slice.299) | copy-start | bytes 884740
  80.7 3.3 %copy-start.41 = (pred[512,1024]{1,0:T(8,128)(4,1)S(1)}, pred[512,1024]{1,0:T(8,128)(4,1)}, u32[]{:S(2)}) copy-start(pred[512,1024]{1,0:T(8,128)(4,1)} %broadcast_compare_fusion) | copy-start | bytes 1572868
  83.9 5.1 %copy-start.39 = (bf16[512,3,48]{0,2,1:T(8,128)(2,1)}, bf16[512,3,48]{0,2,1:T(8,128)(2,1)S(1)}, u32[]{:S(2)}) copy-start(bf16[512,3,48]{0,2,1:T(8,128)(2,1)S(1)} %slice.300) | copy-start | bytes 442372
  84.0 5.0 %copy-start.59 = (bf16[512,3,8]{0,2,1:T(8,128)(2,1)}, bf16[512,3,8]{0,2,1:T(8,128)(2,1)S(1)}, u32[]{:S(2)}) copy-start(bf16[512,3,8]{0,2,1:T(8,128)(2,1)S(1)} %get-tuple-element.69) | copy-start | bytes 73732
  84.0 5.0 %copy-start.61 = (bf16[512,3,8]{0,2,1:T(8,128)(2,1)}, bf16[512,3,8]{0,2,1:T(8,128)(2,1)S(1)}, u32[]{:S(2)}) copy-start(bf16[512,3,8]{0,2,1:T(8,128)(2,1)S(1)} %get-tuple-element.70) | copy-start | bytes 73732
  84.0 5.0 %copy-start.103 = (bf16[1024,3,64]{0,2,1:T(8,128)(2,1)S(1)}, bf16[1024,3,64]{0,2,1:T(8,128)(2,1)}, u32[]{:S(2)}) copy-start(bf16[1024,3,64]{0,2,1:T(8,128)(2,1)} %fusion.22) | copy-start | bytes 1179652
  89.0 4.1 %copy-start.90 = (f32[3,512]{1,0:T(4,128)}, f32[3,512]{1,0:T(4,128)S(1)}, u32[]{:S(2)}) copy-start(f32[3,512]{1,0:T(4,128)S(1)} %get-tuple-element.100) | copy-start | bytes 18436
  89.0 4.1 %copy-start.7 = (bf16[8,1,128,768]{3,2,1,0:T(8,128)(2,1)S(1)}, bf16[8,1,128,768]{3,2,1,0:T(8,128)(2,1)}, u32[]{:S(2)}) copy-start(bf16[8,1,128,768]{3,2,1,0:T(8,128)(2,1)} %slice.183) | copy-start | bytes 4718596
  94.2 4.2 %copy-start.99 = (f32[128]{0:T(128)S(1)}, f32[128]{0:T(128)}, u32[]{:S(2)}) copy-start(f32[128]{0:T(128)} %convert_reduce_fusion.9) | copy-start | bytes 1540
  94.2 4.7 %copy-start.14 = (bf16[1,128,768]{2,1,0:T(8,128)(2,1)S(1)}, bf16[1,128,768]{2,1,0:T(8,128)(2,1)}, u32[]{:S(2)}) copy-start(bf16[1,128,768]{2,1,0:T(8,128)(2,1)} %param.15) | copy-start | bytes 589828
  94.2 5.4 %copy-start.100 = (pred[2]{0:T(512)(128)(4,1)S(1)}, pred[2]{0:T(512)(128)(4,1)}, u32[]{:S(2)}) copy-start(pred[2]{0:T(512)(128)(4,1)} %iota_compare_fusion.1) | copy-start | bytes 10
  94.2 10.4 %copy-start.69 = (f32[32,1,24]{2,1,0:T(1,128)S(1)}, f32[32,1,24]{2,1,0:T(1,128)}, u32[]{:S(2)}) copy-start(f32[32,1,24]{2,1,0:T(1,128)} %get-tuple-element.79) | copy-start | bytes 9220
  94.2 11.0 %copy-start.68 = (f32[32,1,24]{2,1,0:T(1,128)S(1)}, f32[32,1,24]{2,1,0:T(1,128)}, u32[]{:S(2)}) copy-start(f32[32,1,24]{2,1,0:T(1,128)} %get-tuple-element.84) | copy-start | bytes 9220
  97.8 12.0 %copy-start.13 = (bf16[1024,768]{1,0:T(8,128)(2,1)S(1)}, bf16[1024,768]{1,0:T(8,128)(2,1)}, u32[]{:S(2)}) copy-start(bf16[1024,768]{1,0:T(8,128)(2,1)} %get-tuple-element.28) | copy-start | bytes 4718596
  97.8 12.0 %copy-start.49 = (bf16[768,96]{0,1:T(8,128)(2,1)S(1)}, bf16[768,96]{0,1:T(8,128)(2,1)}, u32[]{:S(2)}) copy-start(bf16[768,96]{0,1:T(8,128)(2,1)} %param.21) | copy-start | bytes 442372
  107.5 6.6 %copy-start.51 = (bf16[96,768]{1,0:T(8,128)(2,1)}, bf16[96,768]{1,0:T(8,128)(2,1)S(1)}, u32[]{:S(2)}) copy-start(bf16[96,768]{1,0:T(8,128)(2,1)S(1)} %get-tuple-element.76) | copy-start | bytes 442372
  107.5 8.4 %copy-start.33 = (bf16[96,768]{1,0:T(8,128)(2,1)}, bf16[96,768]{1,0:T(8,128)(2,1)S(1)}, u32[]{:S(2)}) copy-start(bf16[96,768]{1,0:T(8,128)(2,1)S(1)} %get-tuple-element.75) | copy-start | bytes 442372
  108.6 5.5 %copy-start.53 = (bf16[96,768]{1,0:T(8,128)(2,1)}, bf16[96,768]{1,0:T(8,128)(2,1)S(1)}, u32[]{:S(2)}) copy-start(bf16[96,768]{1,0:T(8,128)(2,1)S(1)} %get-tuple-element.74) | copy-start | bytes 442372
  108.7 7.2 %copy-start.35 = (bf16[96,768]{1,0:T(8,128)(2,1)}, bf16[96,768]{1,0:T(8,128)(2,1)S(1)}, u32[]{:S(2)}) copy-start(bf16[96,768]{1,0:T(8,128)(2,1)S(1)} %get-tuple-element.73) | copy-start | bytes 442372
  109.8 4.4 %copy-start.55 = (bf16[96,768]{1,0:T(8,128)(2,1)}, bf16[96,768]{1,0:T(8,128)(2,1)S(1)}, u32[]{:S(2)}) copy-start(bf16[96,768]{1,0:T(8,128)(2,1)S(1)} %get-tuple-element.72) | copy-start | bytes 442372
  109.8 6.1 %copy-start.37 = (bf16[96,768]{1,0:T(8,128)(2,1)}, bf16[96,768]{1,0:T(8,128)(2,1)S(1)}, u32[]{:S(2)}) copy-start(bf16[96,768]{1,0:T(8,128)(2,1)S(1)} %get-tuple-element.71) | copy-start | bytes 442372
  115.0 4.9 %slice-start = ((s8[6291456]{0:T(1024)(128)(4,1)}), s8[4194304]{0:T(1024)(128)(4,1)S(1)}, s32[]{:S(2)}) async-start(s8[6291456]{0:T(1024)(128)(4,1)} %bitcast.231), calls=%async_computation | async-start | bytes 8388608
  115.9 4.0 %slice-start.1 = ((s8[6291456]{0:T(1024)(128)(4,1)}), s8[2097152]{0:T(1024)(128)(4,1)S(1)}, s32[]{:S(2)}) async-start(s8[6291456]{0:T(1024)(128)(4,1)} %bitcast.231), calls=%async_computation.1 | async-start | bytes 4194304
  126.1 6.0 %copy-start.11 = (f32[1024,768]{1,0:T(8,128)S(1)}, f32[1024,768]{1,0:T(8,128)}, u32[]{:S(2)}) copy-start(f32[1024,768]{1,0:T(8,128)} %copy-done.10) | copy-start | bytes 9437188
  129.1 5.0 %copy-start.18 = (f32[1024,3,64]{0,2,1:T(8,128)S(1)}, f32[1024,3,64]{0,2,1:T(8,128)}, u32[]{:S(2)}) copy-start(f32[1024,3,64]{0,2,1:T(8,128)} %fusion.21) | copy-start | bytes 2359300
  139.1 2.2 %copy-start.56 = (bf16[96,768]{1,0:T(8,128)(2,1)S(1)}, bf16[96,768]{1,0:T(8,128)(2,1)}, u32[]{:S(2)}) copy-start(bf16[96,768]{1,0:T(8,128)(2,1)} %copy-done.55) | copy-start | bytes 442372
  139.2 2.2 %copy-start.65 = (f32[768]{0:T(1024)S(1)}, f32[768]{0:T(1024)}, u32[]{:S(2)}) copy-start(f32[768]{0:T(1024)} %copy-done.63) | copy-start | bytes 9220
  139.2 2.2 %copy-start.81 = (f32[1024]{0:T(1024)S(1)}, f32[1024]{0:T(1024)}, u32[]{:S(2)}) copy-start(f32[1024]{0:T(1024)} %get-tuple-element.98) | copy-start | bytes 12292
  139.2 2.2 %copy-start.83 = (f32[1024]{0:T(1024)S(1)}, f32[1024]{0:T(1024)}, u32[]{:S(2)}) copy-start(f32[1024]{0:T(1024)} %get-tuple-element.97) | copy-start | bytes 12292
  139.2 2.2 %copy-start.87 = (f32[768]{0:T(1024)S(1)}, f32[768]{0:T(1024)}, u32[]{:S(2)}) copy-start(f32[768]{0:T(1024)} %mul.325) | copy-start | bytes 9220
  141.4 5.6 %copy-start.23 = (bf16[192,768]{1,0:T(8,128)(2,1)S(1)}, bf16[192,768]{1,0:T(8,128)(2,1)}, u32[]{:S(2)}) copy-start(bf16[192,768]{1,0:T(8,128)(2,1)} %convolution_convert_fusion.5) | copy-start | bytes 884740
  181.6 5.4 %copy-start.3 = (bf16[4,96,768]{2,1,0:T(8,128)(2,1)S(1)}, bf16[4,96,768]{2,1,0:T(8,128)(2,1)}, u32[]{:S(2)}) copy-start(bf16[4,96,768]{2,1,0:T(8,128)(2,1)} %copy-done.2) | copy-start | bytes 1769476
  181.6 6.2 %copy-start.1 = (bf16[4,128,768]{2,1,0:T(8,128)(2,1)S(1)}, bf16[4,128,768]{2,1,0:T(8,128)(2,1)}, u32[]{:S(2)}) copy-start(bf16[4,128,768]{2,1,0:T(8,128)(2,1)} %copy-done) | copy-start | bytes 2359300
  183.2 30.9 %copy-start.101 = (f32[24]{0:T(128)}, f32[24]{0:T(128)S(1)}, u32[]{:S(2)}) copy-start(f32[24]{0:T(128)S(1)} %get-tuple-element.141) | copy-start | bytes 292
  184.4 3.7 %copy-start.15 = (bf16[1,128,768]{2,1,0:T(8,128)(2,1)S(1)}, bf16[1,128,768]{2,1,0:T(8,128)(2,1)}, u32[]{:S(2)}) copy-start(bf16[1,128,768]{2,1,0:T(8,128)(2,1)} %param.15) | copy-start | bytes 589828
  184.4 3.7 %copy-start.97 = (f32[128]{0:T(128)S(1)}, f32[128]{0:T(128)}, u32[]{:S(2)}) copy-start(f32[128]{0:T(128)} %copy-done.96) | copy-start | bytes 1540
  184.4 3.7 %copy-start.98 = (f32[128]{0:T(128)S(1)}, f32[128]{0:T(128)}, u32[]{:S(2)}) copy-start(f32[128]{0:T(128)} %add_rsqrt_fusion.1) | copy-start | bytes 1540
  184.4 15.1 %collective-permute-start.3 = (bf16[192,768]{1,0:T(8,128)(2,1)S(1)}, bf16[192,768]{1,0:T(8,128)(2,1)S(1)}, u32[]{:S(2)}, u32[]{:S(2)}) collective-permute-start(bf16[192,768]{1,0:T(8,128)(2,1)S(1)} %get-tuple-element.55), channel_id=1, source_target_pairs={{0,3},{1,0},{2,1},{3,2},{4,7},{5,4},{6,5},{7,6},{8,11},{9,8},{10,9... | collective-permute-start | bytes 884744 | tf_op jit(solution)/shard_map/ppermute | solution.py:325
  185.5 15.3 %collective-permute-start.5 = (bf16[192,768]{1,0:T(8,128)(2,1)S(1)}, bf16[192,768]{1,0:T(8,128)(2,1)S(1)}, u32[]{:S(2)}, u32[]{:S(2)}) collective-permute-start(bf16[192,768]{1,0:T(8,128)(2,1)S(1)} %get-tuple-element.56), channel_id=1, source_target_pairs={{0,1},{1,2},{2,3},{3,0},{4,5},{5,6},{6,7},{7,4},{8,9},{9,10},{10,1... | collective-permute-start | bytes 884744 | tf_op jit(solution)/shard_map/ppermute | solution.py:325
  186.5 25.6 %collective-permute-start.4 = (bf16[192,768]{1,0:T(8,128)(2,1)S(1)}, bf16[192,768]{1,0:T(8,128)(2,1)S(1)}, u32[]{:S(2)}, u32[]{:S(2)}) collective-permute-start(bf16[192,768]{1,0:T(8,128)(2,1)S(1)} %get-tuple-element.57), channel_id=1, source_target_pairs={{0,2},{1,3},{2,0},{3,1},{4,6},{5,7},{6,4},{7,5},{8,10},{9,11},{10,... | collective-permute-start | bytes 884744 | tf_op jit(solution)/shard_map/ppermute | solution.py:325
  (49 other events, 70.1 us)

commit v3 on v2

--- a/solution.py
+++ b/solution.py
@@ -39,7 +39,7 @@
     return push
 
 
-def gather_kernel(N, F, G, xg, wa, vec, xg_all, wa_all, vec_all, send, recv, local):
+def gather_kernel(N, F, G, xg, wa, wb, vec, xg_all, wa_all, wb_all, vec_all, send, recv, local):
     s, f = lax.axis_index("seq"), lax.axis_index("fsdp")
     grp, g = s // G, lax.rem(s, G)
     partner = (s + 1 - 2 * lax.rem(s, 2), f)
@@ -52,6 +52,7 @@
         pltpu.make_async_copy(xg, xg_all.at[s], local.at[0]),
         pltpu.make_async_copy(wa, wa_all.at[g, f], local.at[1]),
         pltpu.make_async_copy(vec, vec_all.at[s, f], local.at[2]),
+        pltpu.make_async_copy(wb, wb_all.at[f], local.at[3]),
     ]
     for copy in own:
         copy.start()
@@ -59,6 +60,7 @@
     far = [push(xg, xg_all.at[s], (lax.rem(s + k, N), f)) for k in range(2, N, 2)]
     firsts = [push(wa, wa_all.at[g, f], peer) for peer in z_peers]
     rest = [push(xg, xg_all.at[s], partner)]
+    rest += [push(wb, wb_all.at[f], peer) for peer in z_peers]
     for copy in own:
         copy.wait()
     for copy in vecs:
@@ -76,7 +78,7 @@
 
 
 def scatter_kernel(
-    N, F, G, outp, tp, ga, vecp, outr, tr, gar, vecr,
+    N, F, G, outp, tp, ga, gb, vecp, outr, tr, gar, gbr, vecr,
     pair_in, pair_sum, ga_in, ga_sum, vec_in, vec_sum, send, recv
 ):
     s, f = lax.axis_index("seq"), lax.axis_index("fsdp")
@@ -96,8 +98,8 @@
         halves.append(
             [push(a.at[2 * j + 1 - core], pair_in.at[i, j], partner) for i, a in enumerate((outp, tp))]
         )
+    rest = [push(gb.at[p], gbr.at[f], (s, p)) for p in z_index]
     vecs = [push(vecp.at[p], vec_in.at[k], (p, f)) for k, p in enumerate(seq_index)]
-    rest = []
     for copy in mates:
         copy.wait()
     for i in range(F):
@@ -117,6 +119,7 @@
                 pair_sum[i, j] = both
                 waits.append(push(pair_sum.at[i, j], out.at[chip], (2 * j + core, f)))
     gar[f] = ga_sum[f]
+    gbr[f] = gb[f]
     for copy in vecs:
         copy.wait()
     total = vecp[s]
@@ -129,33 +132,30 @@
         copy.wait()
 
 
-COST = pl.CostEstimate(flops=0, bytes_accessed=80 * 10**6, transcendentals=0)
-
-
-def gather_phase(N, F, G, xg, wa, vec):
-    copies = 2 * (F - 1) + 2 * (N - 1) + G - 1
+def gather_phase(N, F, G, xg, wa, wb, vec):
+    copies = 3 * (F - 1) + 2 * (N - 1) + G - 1
     hbm = pl.BlockSpec(memory_space=pl.ANY)
     return pl.pallas_call(
         lambda *refs: gather_kernel(N, F, G, *refs),
         out_shape=(
             jax.ShapeDtypeStruct((N,) + xg.shape, xg.dtype),
             jax.ShapeDtypeStruct((G, F) + wa.shape, wa.dtype),
+            jax.ShapeDtypeStruct((F,) + wb.shape, wb.dtype),
             jax.ShapeDtypeStruct((N, F) + vec.shape, vec.dtype),
         ),
-        in_specs=[hbm] * 3,
-        out_specs=(hbm,) * 3,
+        in_specs=[hbm] * 4,
+        out_specs=(hbm,) * 4,
         scratch_shapes=[
             pltpu.SemaphoreType.DMA((copies,)),
             pltpu.SemaphoreType.DMA((copies,)),
-            pltpu.SemaphoreType.DMA((3,)),
+            pltpu.SemaphoreType.DMA((4,)),
         ],
         compiler_params=pltpu.CompilerParams(collective_id=0, has_side_effects=True),
-        cost_estimate=COST,
-    )(xg, wa, vec)
-
-
-def scatter_phase(N, F, G, outp, tp, ga, vecp):
-    copies = 2 * (F - 1) + 3 * N + G
+    )(xg, wa, wb, vec)
+
+
+def scatter_phase(N, F, G, outp, tp, ga, gb, vecp):
+    copies = 3 * (F - 1) + 3 * N + G
     vmem = pl.BlockSpec(memory_space=pltpu.VMEM)
     half = (N // 2,) + outp.shape[1:]
     return pl.pallas_call(
@@ -164,10 +164,11 @@
             jax.ShapeDtypeStruct(half, BF),
             jax.ShapeDtypeStruct(half, BF),
             jax.ShapeDtypeStruct(ga.shape[1:], BF),
+            jax.ShapeDtypeStruct(gb.shape, BF),
             jax.ShapeDtypeStruct(vecp.shape[1:], F32),
         ),
-        in_specs=[vmem] * 4,
-        out_specs=(vmem,) * 4,
+        in_specs=[vmem] * 5,
+        out_specs=(vmem,) * 5,
         scratch_shapes=[
             pltpu.VMEM((2,) + half, BF),
             pltpu.VMEM((2,) + half, BF),
@@ -181,14 +182,7 @@
         compiler_params=pltpu.CompilerParams(
             collective_id=1, has_side_effects=True, vmem_limit_bytes=48 * 2**20
         ),
-        cost_estimate=COST,
-    )(outp, tp, ga, vecp)
-
-
-def lane_rows(arrays):
-    spread = [jnp.pad(a, [(0, 0)] * (a.ndim - 1) + [(0, 128 - a.shape[-1])]) for a in arrays]
-    spread += [jnp.zeros_like(spread[0])] * (8 - len(spread))
-    return jnp.stack(spread, axis=-2)
+    )(outp, tp, ga, gb, vecp)
 
 
 def row_places(pair_held, count, block_rows):
@@ -241,38 +235,32 @@
         W = HG * HD
         Q = L // G
         cj, cd, ce = joint_weight.shape[1], dense_weight.shape[0], expand_weight.shape[1]
-        s, f = lax.axis_index("seq"), lax.axis_index("fsdp")
+        s = lax.axis_index("seq")
         grp, gi = s // G, s % G
         scale = HD ** (-0.5)
 
         xg = jnp.concatenate([tokens, cotangent], axis=0)
         wa = pad_rows(jnp.concatenate([joint_weight.T, dense_weight], axis=0), 0)
         wb = pad_rows(jnp.concatenate([expand_weight.T, reduce_weight], axis=0), 0)
-        vec = lane_rows(
-            [array.astype(F32) for array in (
+        vec = jnp.concatenate(
+            [jnp.pad(array.astype(F32), (0, 128 - array.shape[0])) for array in (
                 first_gain, first_shift, second_gain, second_shift, joint_bias, dense_bias,
                 expand_bias, reduce_bias)]
-        )
-        wb_list = [wb] + [
-            lax.ppermute(wb, "fsdp", [(i, (i + k) % F) for i in range(F)]) for k in range(1, F)
+        ).reshape(8, 128)
+        xg_all, wa_all, wb_all, vec_all = gather_phase(N, F, G, xg, wa, wb, vec)
+
+        va = vec_all.reshape(N * F, 1024)
+        gain1, shift1, gain2, shift2, _, bias_d, _, bias_r = [
+            va[:, 128 * i:128 * i + cd].reshape(D) for i in range(8)
         ]
-        xg_all, wa_all, vec_all = gather_phase(N, F, G, xg, wa, vec)
-
-        va = vec_all.reshape(N * F, 8, 128)
-        gain1, shift1, gain2, shift2, _, bias_d, _, bias_r = [
-            va[:, i, :cd].reshape(D) for i in range(8)
-        ]
-        bias_j = lax.dynamic_slice_in_dim(va[:, 4, :cj], grp * G * F, G * F, 0).reshape(HG, 3, HD)
-        places_f = jnp.arange(F)
-        turned = (places_f[None, :] == (f - places_f[:, None] + F) % F)[:, :, None]
-        bias_e = lax.dynamic_slice_in_dim(va[:, 6, :ce], s * F, F, 0)
-        bias_e = jnp.sum(jnp.where(turned, bias_e[None], 0.0), axis=1).reshape(F * ce)
+        bias_j = lax.dynamic_slice_in_dim(va[:, 512:512 + cj], grp * G * F, G * F, 0).reshape(HG, 3, HD)
+        bias_e = lax.dynamic_slice_in_dim(va[:, 768:768 + ce], s * F, F, 0).reshape(F * ce)
 
         joint = wa_all[:, :, :cj].reshape(HG, 3, HD, D)
         wq, wk, wv = [joint[:, i].reshape(W, D) for i in range(3)]
         dense = wa_all[:, :, cj:cj + cd].reshape(W, D)
-        expand = jnp.concatenate([w[:ce] for w in wb_list], axis=0)
-        reduce_w = jnp.concatenate([w[ce:2 * ce] for w in wb_list], axis=0)
+        expand = wb_all[:, :ce].reshape(F * ce, D)
+        reduce_w = wb_all[:, ce:2 * ce].reshape(F * ce, D)
 
         x = xg_all[:, 0].reshape(L, D).astype(F32)
         grad = xg_all[:, 1].reshape(L, D)
@@ -310,20 +298,6 @@
         probs = probs_full.astype(BF)
         context = jnp.einsum("hqk,khd->qhd", probs, v, preferred_element_type=F32)
         ctx_low = context.reshape(Q, W).astype(BF)
-        nf2_late, ctx_low = lax.optimization_barrier((nf2, ctx_low))
-        hidden = nt(nf2_late, expand) + bias_e
-        active, gelu_pull = jax.vjp(lambda t: jax.nn.gelu(t, approximate=False), hidden)
-        active = active.astype(BF)
-        g_hidden = gelu_pull(nt(grad, reduce_w))[0].astype(BF)
-        gb = pad_rows(
-            jnp.concatenate(
-                [tn(g_hidden, nf2).astype(BF).reshape(F, ce, D),
-                 tn(active, grad).astype(BF).reshape(F, ce, D)], axis=1), 1
-        )
-        gctx, gb = lax.optimization_barrier((gctx, gb))
-        b_parts = [gb[0]] + [
-            lax.ppermute(gb[k], "fsdp", [(i, (i - k) % F) for i in range(F)]) for k in range(1, F)
-        ]
         g_probs = jnp.einsum("qhd,khd->hqk", gctx, v, preferred_element_type=F32)
         delta = jnp.sum(probs_full * g_probs, axis=-1, keepdims=True)
         g_scores = (probs_full * (g_probs - delta)).astype(BF)
@@ -334,7 +308,11 @@
         gk = turn(gk, cosine, -sine).astype(BF).reshape(L, W)
         gv = gv.astype(BF).reshape(L, W)
 
+        hidden = nt(nf2, expand) + bias_e
+        active, gelu_pull = jax.vjp(lambda t: jax.nn.gelu(t, approximate=False), hidden)
+        active = active.astype(BF)
         out_part = nn(active, reduce_w) + own_rows(nn(ctx_low, dense))
+        g_hidden = gelu_pull(nt(grad, reduce_w))[0].astype(BF)
         g2 = nn(g_hidden, expand)
         g1 = nn(gk, wk) + nn(gv, wv) + own_rows(nn(gq, wq))
         t_part = g1 * gain1 + g2 * gain2
@@ -345,6 +323,11 @@
         ).reshape(G, F, cj, D)
         d_dense = tn(ctx_low, grad_q).astype(BF).reshape(G, F, cd, D)
         ga = pad_rows(jnp.concatenate([d_joint, d_dense], axis=2), 2)
+        gb = pad_rows(
+            jnp.concatenate(
+                [tn(g_hidden, nf2).astype(BF).reshape(F, ce, D),
+                 tn(active, grad).astype(BF).reshape(F, ce, D)], axis=1), 1
+        )
 
         def col(array):
             return jnp.sum(array.astype(F32), axis=0)
@@ -357,15 +340,15 @@
         b_joint = jnp.stack([col(a).reshape(HG, HD) for a in (gq, gk, gv)], axis=1).reshape(G * F, cj)
         b_joint = lax.dynamic_update_slice_in_dim(jnp.zeros((N * F, cj), F32), b_joint, grp * G * F, 0)
         b_expand = lax.dynamic_update_slice_in_dim(
-            jnp.zeros((N * F, ce), F32),
-            jnp.sum(jnp.where(turned, col(g_hidden).reshape(1, F, ce), 0.0), axis=1), s * F, 0
+            jnp.zeros((N * F, ce), F32), col(g_hidden).reshape(F, ce), s * F, 0
         )
         b_out = jnp.where((owner_s == s)[:, None], col(grad).reshape(N * F, cd), 0.0)
-        vecp = lane_rows(gains + [b_joint, b_out, b_expand]).reshape(N, F, 8, 128)
-
-        outr, tr, gar, vecr = scatter_phase(
+        vecp = jnp.concatenate(gains + [b_joint, b_out, b_expand], axis=1)
+        vecp = jnp.pad(vecp, ((0, 0), (0, 1024 - vecp.shape[1]))).reshape(N, F, 8, 128)
+
+        outr, tr, gar, gbr, vecr = scatter_phase(
             N, F, G, out_part.astype(BF).reshape(N, R, D), t_part.astype(BF).reshape(N, R, D),
-            ga, vecp
+            ga, gb, vecp
         )
         x_own = tokens[0].astype(F32)
         layer_output = (x_own + jnp.sum(outr.astype(F32), axis=0) + bias_d + bias_r).astype(BF)
@@ -379,13 +362,16 @@
         ) * inv_own
         input_grad = (cotangent[0].astype(F32) + g_in).astype(BF)
         a = jnp.sum(gar.astype(F32), axis=0)
-        b = sum(part.astype(F32) for part in b_parts)
-        vs = jnp.sum(vecr, axis=0)
-        o_joint, o_out, o_expand = vs[4, :cj], vs[5, :cd], vs[6, :ce]
+        b = jnp.sum(gbr.astype(F32), axis=0)
+        vs = jnp.sum(vecr, axis=0).reshape(1024)
+        at = 4 * cd
+        o_joint, at = vs[at:at + cj], at + cj
+        o_out, at = vs[at:at + cd], at + cd
+        o_expand = vs[at:at + ce]
         return (
             layer_output[None], input_grad[None], a[:cj].T, o_joint, a[cj:cj + cd], o_out,
             b[:ce].T, o_expand, b[ce:2 * ce], o_out,
-            vs[0, :cd], vs[1, :cd], vs[2, :cd], vs[3, :cd],
+            vs[:cd], vs[cd:2 * cd], vs[2 * cd:3 * cd], vs[3 * cd:4 * cd],
         )
 
     return body

time: 216 us -> 185 us (0.86)
  Pallas kernels: 61.4 us -> 89.8 us
  waiting for transfers between devices: 22.1 us -> 0 us
  local copies, waits for them, and re-layouts: 48.9 us -> 28.3 us
  starting transfers between devices: 8.71 us -> 0 us
  matrix products: 42.7 us -> 38.8 us
  other arithmetic: 28.8 us -> 25.6 us
    ppermute x6 -> x0, waiting for transfers between devices: 22.1 us -> none  [the longest x3 22.1 us: body(): lax.ppermute(gb[k], 'fsdp', [(i, (i - k) % F) for i in range(F)])]
    pallas_call x1, Pallas kernels: 29.8 us -> 49 us  [scatter_phase(): pl.pallas_call(lambda *refs: scatter_kernel(N, F, G, *refs), out_shape=(j...]
    pallas_call x1, Pallas kernels: 31.6 us -> 40.8 us  [gather_phase(): pl.pallas_call(lambda *refs: gather_kernel(N, F, G, *refs), out_shape=(ja...]
    ppermute x6 -> x0, starting transfers between devices: 8.71 us -> none  [the longest x3 6.06 us: body(): lax.ppermute(wb, 'fsdp', [(i, (i + k) % F) for i in range(F)])]
    slice x6 -> x7, local copies, waits for them, and re-layouts: 7.84 us -> 1.84 us  [the longest x1 0.59 us: body(): vs[3 * cd:4 * cd]]
    another operation x7 -> x0, local copies, waits for them, and re-layouts: 3.59 us -> none  [lane_rows(): return jnp.stack(spread, axis=-2)]
    squeeze x4 -> x0, local copies, waits for them, and re-layouts: 2.75 us -> none  [the longest x1 1.2 us: body(): gb[k]]
    unnamed x218 -> x151, local copies, waits for them, and re-layouts: 10.9 us -> 13.2 us
  transfers between devices with their start and end apart: 6 -> 0, of which waited for: 3 -> 0; matrix products, arithmetic and copies ran while one was open for 32% -> 0% of each run, Pallas kernels for 15% -> 0%
where the time goes in v3:
time: 185 us; the launch traced here: 184 us
  Pallas kernels  89.8 us (49%)
  matrix products  38.8 us (21%)
  local copies, waits for them, and re-layouts  28.3 us (15%)
  other arithmetic  25.6 us (14%)
    pallas_call x1, Pallas kernels, scatter_phase(): pl.pallas_call(lambda *refs: scatter_kernel(N, F, G, *refs), out_shape=(j...  49 us
    pallas_call x1, Pallas kernels, gather_phase(): pl.pallas_call(lambda *refs: gather_kernel(N, F, G, *refs), out_shape=(ja...  40.8 us
    unnamed x151, local copies, waits for them, and re-layouts  13.2 us
    dot_general x6, matrix products, nt(): lax.dot_general(left, right, (((1,), (1,)), ((), ())), preferred_element_...  11.3 us
    dot_general x6, matrix products, nn(): return jnp.dot(left, right, preferred_element_type=F32)  9.11 us
    pad x8, local copies, waits for them, and re-layouts, body(): jnp.pad(array.astype(F32), (0, 128 - array.shape[0]))  5.38 us
    dot_general x6, matrix products, tn(): lax.dot_general(left, right, (((0,), (0,)), ((), ())), preferred_element_...  4.97 us
    sub x1, matrix products, body(): weight = jnp.exp(scores - peak)  4.95 us

profile of v3, /device:TPU:0, one launch (start us, length us, event | category | flops | bytes accessed | tf_op | source)
XLA Modules:
  0.0 184.3 jit_solution(18069035266916130974)
XLA Ops:
  0.7 0.8 pad.43
  1.5 0.7 pad.44
  2.2 0.7 pad.45
  2.8 0.7 pad.46
  3.5 0.7 pad.39
  4.1 0.7 pad.40
  4.8 0.7 pad.41
  5.5 0.7 pad.42
  6.1 0.7 subtract_bitcast_fusion
  6.8 0.7 add_multiply_fusion
  7.4 1.0 convert_reduce_fusion.10
  8.5 1.1 fusion.51
  13.3 0.8 fusion.59
  14.8 1.6 pad_maximum_fusion.8.refs_1_
  16.3 1.7 pad_maximum_fusion.6.refs_2_
  18.1 0.8 pad_maximum_fusion.3.refs_0_
  18.8 1.2 broadcast_compare_fusion
  20.0 40.8 %shard_map.254 = (bf16[8,2,128,768]{3,2,1,0:T(8,128)(2,1)}, bf16[2,4,96,768]{3,2,1,0:T(8,128)(2,1)}, bf16[4,192,768]{2,1,0:T(8,128)(2,1)}, f32[8,4,8,128]{3,2,1,0:T(8,128)}) custom-call(bf16[2,128,768]{2,1,0:T(8,128)(2,1)} %pad_maximum_fusion.3.refs_0_, bf16[96,768]{1,0:T(8,128)(2,1)} %pad_maximum_fusion.8.refs_1_, ...), custom_call_target="tpu_custom_call" | custom-call | tf_op jit(solution)/shard_map/pallas_call | solution.py:138
  60.9 0.9 copy.55
  61.8 1.7 convert_reduce_fusion.1
  64.1 2.8 %convert_reduce_fusion = (f32[768]{0:T(1024)S(1)}, f32[8,128]{1,0:T(8,128)S(1)}) fusion(bf16[8,2,128,768]{3,2,1,0:T(8,128)(2,1)} %get-tuple-element.23, f32[8,128]{1,0:T(8,128)S(1)} %get-tuple-element.87), kind=kLoop, calls=%fused_computation.13 | loop fusion | flops 4716800 | bytes 3156992 | tf_op jit(solution)/shard_map/reduce_sum | solution.py:333
  67.5 0.7 broadcast_select_fusion
  68.3 0.7 add.260
  70.1 0.7 add.263
  70.8 1.0 fusion.75
  71.8 0.9 copy-done.24
  72.8 0.9 copy-done.3
  73.8 1.2 convolution_convert_fusion.5
  75.0 0.9 add_convert_fusion.2
  75.9 1.0 convolution_add_fusion
  76.9 1.4 fusion.26
  78.3 0.7 convolution_add_fusion.1
  79.0 0.7 subtract_convert_fusion.1
  79.6 0.8 slice.249
  80.4 5.2 %convert_reduce_fusion.6 = (f32[384]{0:T(512)S(1)}, bf16[1024,384]{1,0:T(8,128)(2,1)}, f32[1024,384]{1,0:T(8,128)S(1)}) fusion(f32[1024,384]{1,0:T(8,128)S(1)} %convolution_add_fusion, bf16[1024,768]{1,0:T(8,128)(2,1)S(1)} %bitcast.169, bf16[384,768]{1,0:T(8,128)(2,1)S(1)} %bitcast.186), kind=kOutput, calls=%fused_computation.36 | convolution fusion | flops 633077376 | bytes 6096384 | tf_op jit(solution)/shard_map/dot_general | solution.py:204
  85.6 1.2 multiply_convert_fusion.1
  86.9 2.5 %convolution_convert_fusion = bf16[384,768]{1,0:T(8,128)(2,1)S(1)} fusion(bf16[1024,384]{1,0:T(8,128)(2,1)} %multiply_convert_fusion.1, bf16[1024,768]{1,0:T(8,128)(2,1)} %bitcast.170), kind=kOutput, calls=%fused_computation.60 | convolution fusion | flops 604274688 | bytes 2949120 | tf_op jit(solution)/shard_map/dot_general | solution.py:212
  90.1 1.8 convolution_add_fusion.3
  92.2 0.8 fusion.24
  93.2 0.8 copy-done.25
  94.2 4.9 %fusion.80 = (f32[3,512]{1,0:T(4,128)S(1)}, f32[3,512,1024]{2,1,0:T(8,128)}) fusion(pred[512,1024]{1,0:T(8,128)(4,1)S(1)} %copy-done.30, bf16[512,3,48]{0,2,1:T(8,128)(2,1)S(1)} %slice.250, bf16[512,3,8]{0,2,1:T(8,128)(2,1)S(1)} %get-tuple-element.66, bf16[512,3,8]{0,2,1:T(8,128)(2,1)S(1)} %get-tuple-element.65, bf16[1024,3,48]{0,2,1:T(8,128)(2,1)S(1)} %copy-done.25, ...), kind=kOutput, calls=%fused_computation.182 | convolution fusion | flops 209388544 | bytes 7411712 | tf_op jit(solution)/shard_map/sub | solution.py:296
  99.2 4.1 %fusion.31 = bf16[3,64,512]{2,1,0:T(8,128)(2,1)S(1)} fusion(bf16[1024,3,64]{0,2,1:T(8,128)(2,1)S(1)} %copy-done.67, f32[3,512,1024]{2,1,0:T(8,128)} %get-tuple-element.91, f32[3,512]{1,0:T(4,128)S(1)} %get-tuple-element.90), kind=kOutput, calls=%fused_computation.77 | convolution fusion | flops 204570624 | bytes 6887424 | tf_op jit(solution)/shard_map/hqk,khd->qhd/dot_general | solution.py:299
  103.7 0.6 copy-done.12
  104.3 0.9 convert_reduce_fusion.8
  106.7 0.7 copy-done.11
  107.5 2.2 %fusion.4 = bf16[1024,768]{1,0:T(8,128)(2,1)} fusion(bf16[1024,384]{1,0:T(8,128)(2,1)S(1)} %copy-done.11, bf16[384,768]{1,0:T(8,128)(2,1)S(1)} %bitcast.187, f32[512,768]{1,0:T(8,128)S(1)} %fusion.81, pred[1024]{0:T(1024)(128)(4,1)S(1)} %copy-done.56), kind=kOutput, calls=%fused_computation.10 | convolution fusion | flops 606339072 | bytes 4523008 | tf_op jit(solution)/shard_map/dot_general | solution.py:208
  109.7 1.8 multiply_reduce_fusion
  111.5 1.3 multiply_convert_fusion
  112.7 1.1 fusion.30
  113.9 0.7 fusion.25
  114.7 1.0 copy-done.10
  117.4 1.4 fusion.83
  118.8 1.6 fusion.82
  120.6 0.7 fusion.2
  121.3 1.1 copy-done.4
  122.8 2.8 %multiply_reduce_fusion.1 = (f32[768]{0:T(1024)S(1)}, f32[768]{0:T(1024)S(1)}, f32[768]{0:T(1024)S(1)}, f32[768]{0:T(1024)S(1)}, bf16[1024,768]{1,0:T(8,128)(2,1)}) fusion(f32[1024]{0:T(1024)S(1)} %copy-done.50, f32[1024]{0:T(1024)S(1)} %copy-done.48, bf16[8,2,128,768]{3,2,1,0:T(8,128)(2,1)S(1)} %copy-done.4, f32[1024,768]{1,0:T(8,128)S(1)} %fusion.2, ...), kind=kOutput, calls=%fused_computation.14 | convolution fusion | flops 614200320 | bytes 7694336 | tf_op jit(solution)/shard_map/dot_general | solution.py:208
  126.1 49.0 %shard_map.255 = (bf16[4,128,768]{2,1,0:T(8,128)(2,1)S(1)}, bf16[4,128,768]{2,1,0:T(8,128)(2,1)S(1)}, bf16[4,96,768]{2,1,0:T(8,128)(2,1)S(1)}, bf16[4,192,768]{2,1,0:T(8,128)(2,1)S(1)}, f32[4,8,128]{2,1,0:T(8,128)S(1)}) custom-call(bf16[8,128,768]{2,1,0:T(8,128)(2,1)} %bitcast.176, bf16[8,128,768]{2,1,0:T(8,128)(2,1)} %bitcast.193, ...), custom_call_target="tpu_custom_call" | custom-call | tf_op jit(solution)/shard_map/pallas_call | solution.py:161
  175.0 0.9 copy-done
  175.9 0.8 copy-done.2
  178.7 1.2 convert_reduce_fusion.7
  179.9 0.6 slice.202
  180.6 0.7 slice_bitcast_fusion.1
  181.8 0.9 fusion.47
  182.9 0.8 fusion.76
  (219 shorter events, 15.9 us)
Async XLA Ops:
  0.6 17.4 %copy-start.13 = (bf16[1,128,768]{2,1,0:T(8,128)(2,1)S(1)}, bf16[1,128,768]{2,1,0:T(8,128)(2,1)}, u32[]{:S(2)}) copy-start(bf16[1,128,768]{2,1,0:T(8,128)(2,1)} %param.15) | copy-start | bytes 589828
  0.7 17.4 %copy-start.26 = (bf16[1,128,768]{2,1,0:T(8,128)(2,1)S(1)}, bf16[1,128,768]{2,1,0:T(8,128)(2,1)}, u32[]{:S(2)}) copy-start(bf16[1,128,768]{2,1,0:T(8,128)(2,1)} %param.29) | copy-start | bytes 589828
  8.5 1.7 copy-start.61
  64.1 6.6 %copy-start.23 = (bf16[2,4,96,768]{3,2,1,0:T(8,128)(2,1)S(1)}, bf16[2,4,96,768]{3,2,1,0:T(8,128)(2,1)}, u32[]{:S(2)}) copy-start(bf16[2,4,96,768]{3,2,1,0:T(8,128)(2,1)} %get-tuple-element.26) | copy-start | bytes 3538948
  69.8 5.2 %copy-start.35 = (f32[768]{0:T(1024)}, f32[768]{0:T(1024)S(1)}, u32[]{:S(2)}) copy-start(f32[768]{0:T(1024)S(1)} %mul.338) | copy-start | bytes 9220
  69.9 5.1 %copy-start.38 = (f32[768]{0:T(1024)}, f32[768]{0:T(1024)S(1)}, u32[]{:S(2)}) copy-start(f32[768]{0:T(1024)S(1)} %add.229) | copy-start | bytes 9220
  70.0 5.0 %copy-start.51 = (f32[768]{0:T(1024)}, f32[768]{0:T(1024)S(1)}, u32[]{:S(2)}) copy-start(f32[768]{0:T(1024)S(1)} %mul.331) | copy-start | bytes 9220
  70.1 4.9 %copy-start.54 = (f32[768]{0:T(1024)}, f32[768]{0:T(1024)S(1)}, u32[]{:S(2)}) copy-start(f32[768]{0:T(1024)S(1)} %add.221) | copy-start | bytes 9220
  70.7 1.9 %copy-start.24 = (bf16[4,192,768]{2,1,0:T(8,128)(2,1)S(1)}, bf16[4,192,768]{2,1,0:T(8,128)(2,1)}, u32[]{:S(2)}) copy-start(bf16[4,192,768]{2,1,0:T(8,128)(2,1)} %get-tuple-element.25) | copy-start | bytes 3538948
  70.8 7.5 %copy-start.15 = (bf16[2,4,72,768]{3,2,1,0:T(8,128)(2,1)}, bf16[2,4,72,768]{3,2,1,0:T(8,128)(2,1)S(1)}, u32[]{:S(2)}) copy-start(bf16[2,4,72,768]{3,2,1,0:T(8,128)(2,1)S(1)} %slice.140) | copy-start | bytes 2654212
  70.8 2.8 %copy-start.3 = (bf16[8,2,128,768]{3,2,1,0:T(8,128)(2,1)S(1)}, bf16[8,2,128,768]{3,2,1,0:T(8,128)(2,1)}, u32[]{:S(2)}) copy-start(bf16[8,2,128,768]{3,2,1,0:T(8,128)(2,1)} %get-tuple-element.23) | copy-start | bytes 9437188
  72.7 3.1 %copy-start.28 = (bf16[4,96,768]{2,1,0:T(8,128)(2,1)}, bf16[4,96,768]{2,1,0:T(8,128)(2,1)S(1)}, u32[]{:S(2)}) copy-start(bf16[4,96,768]{2,1,0:T(8,128)(2,1)S(1)} %get-tuple-element.52) | copy-start | bytes 1769476
  72.7 7.6 %copy-start.18 = (bf16[4,96,768]{2,1,0:T(8,128)(2,1)}, bf16[4,96,768]{2,1,0:T(8,128)(2,1)S(1)}, u32[]{:S(2)}) copy-start(bf16[4,96,768]{2,1,0:T(8,128)(2,1)S(1)} %get-tuple-element.53) | copy-start | bytes 1769476
  73.7 6.6 %copy-start.5 = (bf16[8,1,128,768]{3,2,1,0:T(8,128)(2,1)}, bf16[8,1,128,768]{3,2,1,0:T(8,128)(2,1)S(1)}, u32[]{:S(2)}) copy-start(bf16[8,1,128,768]{3,2,1,0:T(8,128)(2,1)S(1)} %slice.155) | copy-start | bytes 4718596
  75.9 2.5 %copy-start.7 = (bf16[8,1,128,768]{3,2,1,0:T(8,128)(2,1)}, bf16[8,1,128,768]{3,2,1,0:T(8,128)(2,1)S(1)}, u32[]{:S(2)}) copy-start(bf16[8,1,128,768]{3,2,1,0:T(8,128)(2,1)S(1)} %get-tuple-element.50) | copy-start | bytes 4718596
  86.8 2.6 %copy-start.47 = (f32[1024]{0:T(1024)S(1)}, f32[1024]{0:T(1024)}, u32[]{:S(2)}) copy-start(f32[1024]{0:T(1024)} %get-tuple-element.86) | copy-start | bytes 12292
  86.8 2.6 %copy-start.49 = (f32[1024]{0:T(1024)S(1)}, f32[1024]{0:T(1024)}, u32[]{:S(2)}) copy-start(f32[1024]{0:T(1024)} %get-tuple-element.88) | copy-start | bytes 12292
  86.9 2.5 %copy-start.41 = (f32[32,96]{1,0:T(8,128)}, f32[32,96]{1,0:T(8,128)S(1)}, u32[]{:S(2)}) copy-start(f32[32,96]{1,0:T(8,128)S(1)} %constant_dynamic-update-slice_fusion) | copy-start | bytes 36868
  90.1 3.0 %copy-start.9 = (f32[1024,768]{1,0:T(8,128)}, f32[1024,768]{1,0:T(8,128)S(1)}, u32[]{:S(2)}) copy-start(f32[1024,768]{1,0:T(8,128)S(1)} %fusion.5) | copy-start | bytes 9437188
  90.1 1.8 copy-start.33
  90.1 1.8 copy-start.44
  90.1 1.9 %copy-start.52 = (f32[768]{0:T(1024)S(1)}, f32[768]{0:T(1024)}, u32[]{:S(2)}) copy-start(f32[768]{0:T(1024)} %copy-done.51) | copy-start | bytes 9220
  90.1 1.9 %copy-start.55 = (f32[768]{0:T(1024)S(1)}, f32[768]{0:T(1024)}, u32[]{:S(2)}) copy-start(f32[768]{0:T(1024)} %copy-done.54) | copy-start | bytes 9220
  90.1 2.1 %copy-start.65 = (bf16[1024,384]{1,0:T(8,128)(2,1)S(1)}, bf16[1024,384]{1,0:T(8,128)(2,1)}, u32[]{:S(2)}) copy-start(bf16[1024,384]{1,0:T(8,128)(2,1)} %get-tuple-element.41) | copy-start | bytes 2359300
  93.1 1.0 copy-start.25
  93.1 1.1 copy-start.30
  93.1 1.1 copy-start.31
  94.2 5.0 %copy-start.67 = (bf16[1024,3,64]{0,2,1:T(8,128)(2,1)S(1)}, bf16[1024,3,64]{0,2,1:T(8,128)(2,1)}, u32[]{:S(2)}) copy-start(bf16[1024,3,64]{0,2,1:T(8,128)(2,1)} %fusion.26) | copy-start | bytes 1179652
  99.2 4.5 %copy-start.58 = (f32[3,512]{1,0:T(4,128)}, f32[3,512]{1,0:T(4,128)S(1)}, u32[]{:S(2)}) copy-start(f32[3,512]{1,0:T(4,128)S(1)} %get-tuple-element.90) | copy-start | bytes 18436
  99.2 4.1 %copy-start.6 = (bf16[8,1,128,768]{3,2,1,0:T(8,128)(2,1)S(1)}, bf16[8,1,128,768]{3,2,1,0:T(8,128)(2,1)}, u32[]{:S(2)}) copy-start(bf16[8,1,128,768]{3,2,1,0:T(8,128)(2,1)} %copy-done.5) | copy-start | bytes 4718596
  99.2 5.1 %copy-start.12 = (f32[3,512,1024]{2,1,0:T(8,128)S(1)}, f32[3,512,1024]{2,1,0:T(8,128)}, u32[]{:S(2)}) copy-start(f32[3,512,1024]{2,1,0:T(8,128)} %get-tuple-element.91) | copy-start | bytes 18874372
  99.2 5.1 %copy-start.32 = (bf16[512,192]{0,1:T(8,128)(2,1)S(1)}, bf16[512,192]{0,1:T(8,128)(2,1)}, u32[]{:S(2)}) copy-start(bf16[512,192]{0,1:T(8,128)(2,1)} %convolution_convert_fusion.5) | copy-start | bytes 589828
  104.3 1.4 copy-start.8
  105.2 1.5 copy-start.20
  106.2 1.1 copy-start.11
  106.2 1.3 copy-start.19
  106.2 1.3 copy-start.56
  107.5 2.2 %copy-start.59 = (f32[3,512]{1,0:T(4,128)S(1)}, f32[3,512]{1,0:T(4,128)}, u32[]{:S(2)}) copy-start(f32[3,512]{1,0:T(4,128)} %copy-done.58) | copy-start | bytes 18436
  107.5 2.2 %copy-start.68 = (bf16[1024,3,64]{0,2,1:T(8,128)(2,1)S(1)}, bf16[1024,3,64]{0,2,1:T(8,128)(2,1)}, u32[]{:S(2)}) copy-start(bf16[1024,3,64]{0,2,1:T(8,128)(2,1)} %fusion.26) | copy-start | bytes 1179652
  113.9 1.9 %copy-start.10 = (f32[1024,768]{1,0:T(8,128)S(1)}, f32[1024,768]{1,0:T(8,128)}, u32[]{:S(2)}) copy-start(f32[1024,768]{1,0:T(8,128)} %copy-done.9) | copy-start | bytes 9437188
  114.6 1.5 copy-start.34
  117.3 1.5 copy-start.17
  118.8 1.7 copy-start.21
  118.8 1.7 copy-start.22
  118.8 1.7 copy-start.57
  120.5 1.9 %copy-start.4 = (bf16[8,2,128,768]{3,2,1,0:T(8,128)(2,1)S(1)}, bf16[8,2,128,768]{3,2,1,0:T(8,128)(2,1)}, u32[]{:S(2)}) copy-start(bf16[8,2,128,768]{3,2,1,0:T(8,128)(2,1)} %get-tuple-element.23) | copy-start | bytes 9437188
  120.5 2.0 %copy-start.29 = (bf16[4,96,768]{2,1,0:T(8,128)(2,1)S(1)}, bf16[4,96,768]{2,1,0:T(8,128)(2,1)}, u32[]{:S(2)}) copy-start(bf16[4,96,768]{2,1,0:T(8,128)(2,1)} %copy-done.28) | copy-start | bytes 1769476
  120.5 2.0 %copy-start.37 = (f32[768]{0:T(1024)S(1)}, f32[768]{0:T(1024)}, u32[]{:S(2)}) copy-start(f32[768]{0:T(1024)} %copy-done.35) | copy-start | bytes 9220
  120.5 2.0 %copy-start.48 = (f32[1024]{0:T(1024)S(1)}, f32[1024]{0:T(1024)}, u32[]{:S(2)}) copy-start(f32[1024]{0:T(1024)} %get-tuple-element.86) | copy-start | bytes 12292
  120.6 2.0 %copy-start.50 = (f32[1024]{0:T(1024)S(1)}, f32[1024]{0:T(1024)}, u32[]{:S(2)}) copy-start(f32[1024]{0:T(1024)} %get-tuple-element.88) | copy-start | bytes 12292
  120.6 2.0 %copy-start.53 = (f32[768]{0:T(1024)S(1)}, f32[768]{0:T(1024)}, u32[]{:S(2)}) copy-start(f32[768]{0:T(1024)} %copy-done.51) | copy-start | bytes 9220
  120.6 2.2 %copy-start.66 = (bf16[1024,384]{1,0:T(8,128)(2,1)S(1)}, bf16[1024,384]{1,0:T(8,128)(2,1)}, u32[]{:S(2)}) copy-start(bf16[1024,384]{1,0:T(8,128)(2,1)} %get-tuple-element.41) | copy-start | bytes 2359300
  122.8 3.1 %copy-start.40 = (f32[32,24]{1,0:T(8,128)S(1)}, f32[32,24]{1,0:T(8,128)}, u32[]{:S(2)}) copy-start(f32[32,24]{1,0:T(8,128)} %broadcast_select_fusion) | copy-start | bytes 9220
  122.8 3.1 %copy-start.42 = (f32[32,96]{1,0:T(8,128)S(1)}, f32[32,96]{1,0:T(8,128)}, u32[]{:S(2)}) copy-start(f32[32,96]{1,0:T(8,128)} %copy-done.41) | copy-start | bytes 36868
  175.0 0.9 copy-start
  175.9 0.8 copy-start.2
  176.8 4.5 %copy-start.1 = (bf16[4,128,768]{2,1,0:T(8,128)(2,1)S(1)}, bf16[4,128,768]{2,1,0:T(8,128)(2,1)}, u32[]{:S(2)}) copy-start(bf16[4,128,768]{2,1,0:T(8,128)(2,1)} %copy-done) | copy-start | bytes 2359300
  176.9 4.6 %copy-start.14 = (bf16[1,128,768]{2,1,0:T(8,128)(2,1)S(1)}, bf16[1,128,768]{2,1,0:T(8,128)(2,1)}, u32[]{:S(2)}) copy-start(bf16[1,128,768]{2,1,0:T(8,128)(2,1)} %param.15) | copy-start | bytes 589828
  176.9 4.6 %copy-start.62 = (f32[128]{0:T(128)S(1)}, f32[128]{0:T(128)}, u32[]{:S(2)}) copy-start(f32[128]{0:T(128)} %copy-done.61) | copy-start | bytes 1540
  176.9 4.6 %copy-start.63 = (f32[128]{0:T(128)S(1)}, f32[128]{0:T(128)}, u32[]{:S(2)}) copy-start(f32[128]{0:T(128)} %add_rsqrt_fusion.1) | copy-start | bytes 1540
  178.7 5.1 %copy-start.64 = (f32[24]{0:T(128)}, f32[24]{0:T(128)S(1)}, u32[]{:S(2)}) copy-start(f32[24]{0:T(128)S(1)} %get-tuple-element.122) | copy-start | bytes 292
  178.7 3.1 %copy-start.27 = (bf16[1,128,768]{2,1,0:T(8,128)(2,1)S(1)}, bf16[1,128,768]{2,1,0:T(8,128)(2,1)}, u32[]{:S(2)}) copy-start(bf16[1,128,768]{2,1,0:T(8,128)(2,1)} %param.29) | copy-start | bytes 589828
  178.7 3.1 %copy-start.45 = (f32[768]{0:T(1024)S(1)}, f32[768]{0:T(1024)}, u32[]{:S(2)}) copy-start(f32[768]{0:T(1024)} %add.260) | copy-start | bytes 9220
  178.7 3.1 %copy-start.46 = (f32[768]{0:T(1024)S(1)}, f32[768]{0:T(1024)}, u32[]{:S(2)}) copy-start(f32[768]{0:T(1024)} %add.263) | copy-start | bytes 9220
  (5 other events, 3.5 us)
